TPU v7x, 256 devices: a whole 4x4x8 slice. The times are simulated.
256 devices in a mesh: node: 32 (over z, y_hi, core), local: 8 (over y_lo, x).
Axes of the slice: x: 4, y: 4 (y_hi: 2, y_lo: 2; y = y_hi * 2 + y_lo), z: 8, core: 2. Of those that a mesh axis runs over, the one named last changes fastest.
Arguments:
- out_grad: bfloat16 [15360, 4096], P('node', 'local'), may hold values from -0.375 to 0.375
- gate_pre: bfloat16 [15360, 14336], P('node', 'local'), may hold values from -8 to 8
- up_pre: bfloat16 [15360, 14336], P('node', 'local'), may hold values from -6 to 6
- down_tiles: bfloat16 [4096, 14336], P('node', 'local'), may hold values from -4 to 4
- down_scales: float32 [32, 112], P('node', 'local'), may hold values from 0.19364917 to 1.9364917
Outputs:
- gate_grad: bfloat16 [15360, 14336], P('node', 'local')
- up_grad: bfloat16 [15360, 14336], P('node', 'local')
- down_grad: float32 [4096, 14336], P('node', 'local')
All inputs are finite; a program needn't handle non-finite values.
Results may differ from a plain program's by a relative error of at most 0.019.
Values may be sent and summed in bfloat16 or wider, within the bound.
No kernel may reach another device: no remote copies, remote signals or barrier semaphores. Data moves between devices by JAX's collectives and lax.ppermute only.
A program may use at most 128 MiB of HBM per device.

v0:
```python
import jax
import jax.numpy as jnp
from jax import lax
from jax.sharding import PartitionSpec as P


def dequantize(tiles, scales):
    rows, cols = tiles.shape
    side = rows // scales.shape[0]
    blocks = tiles.astype(jnp.float32).reshape(rows // side, side, cols // side, side)
    return (blocks * scales[:, None, :, None]).reshape(rows, cols).astype(jnp.bfloat16)


def per_device(out_grad, gate_pre, up_pre, down_tiles, down_scales):
    full_grad = lax.all_gather(out_grad, "local", axis=1, tiled=True)
    gate = gate_pre.astype(jnp.float32)
    up = up_pre.astype(jnp.float32)
    sig = jax.nn.sigmoid(gate)
    swish = gate * sig
    hidden = (swish * up).astype(jnp.bfloat16)
    weight = dequantize(down_tiles, down_scales)
    columns = full_grad
    hidden_grad = jnp.dot(
        columns,
        lax.all_gather(weight, "node", axis=0, tiled=True),
        preferred_element_type=jnp.float32,
    )
    columns = full_grad
    down_grad = lax.psum_scatter(
        lax.dot_general(
            columns, hidden, (((0,), (0,)), ((), ())), preferred_element_type=jnp.float32
        ).astype(jnp.bfloat16),
        "node",
        scatter_dimension=0,
        tiled=True,
    ).astype(jnp.float32)
    gate_grad = (hidden_grad * up * sig * (1.0 + gate * (1.0 - sig))).astype(jnp.bfloat16)
    up_grad = (hidden_grad * swish).astype(jnp.bfloat16)
    return (gate_grad, up_grad, down_grad)


def solution(mesh):
    return jax.shard_map(
        per_device,
        mesh=mesh,
        in_specs=(
            P("node", "local"),
            P("node", "local"),
            P("node", "local"),
            P("node", "local"),
            P("node", "local"),
        ),
        out_specs=(P("node", "local"), P("node", "local"), P("node", "local")),
        check_vma=False,
    )
```

profile of v0, /device:TPU:1, one launch (start us, length us, event | category | flops | bytes accessed | tf_op | source)
XLA Modules:
  0.0 386.8 jit_solution(7752399074287089423)
XLA Ops:
  7.2 0.0 copy-start
  7.2 0.0 all-gather.5.cloned.1.call-start
  7.2 0.7 all-gather.5.cloned.1.call-update
  7.9 0.0 all-gather.3.cloned.1.call-start
  8.0 0.0 copy-done
  8.0 0.1 broadcast_bitcast_fusion
  8.0 1.9 multiply_convert_fusion
  9.9 0.0 all-gather.3.cloned.1.call-update
  9.9 0.0 reduce-scatter.4.cloned.1.call-start
  10.0 56.3 %all-gather.5.cloned.1.call-done = bf16[480,4096]{1,0:T(8,128)(2,1)} async-done(((bf16[480,512]{1,0:T(8,128)(2,1)}), bf16[480,4096]{1,0:T(8,128)(2,1)}) %all-gather.5.cloned.1.call-update) | async-done | bytes 3932176 | tf_op jit(solution)/shard_map/all_gather | solution.py:15
  66.3 14.0 %fusion = bf16[4096,1792]{0,1:T(8,128)(2,1)} fusion(bf16[480,4096]{1,0:T(8,128)(2,1)} %all-gather.5.cloned.1.call-done, bf16[480,1792]{1,0:T(8,128)(2,1)} %param.7, bf16[480,1792]{1,0:T(8,128)(2,1)} %param.6), kind=kOutput, calls=%fused_computation.1 | convolution fusion | flops 7060652032 | bytes 22052864 | tf_op jit(solution)/shard_map/dot_general | solution.py:30
  80.3 18.8 %copy.10 = bf16[4096,1792]{1,0:T(8,128)(2,1)} copy(bf16[4096,1792]{0,1:T(8,128)(2,1)} %fusion) | data formatting | bytes 29360128
  99.1 0.0 copy-start.1
  99.1 0.0 copy-start.2
  99.1 0.0 reduce-scatter.4.cloned.1.call-update
  99.1 97.4 %all-gather.3.cloned.1.call-done = bf16[4096,1792]{1,0:T(8,128)(2,1)} async-done(((bf16[128,1792]{1,0:T(8,128)(2,1)}), bf16[4096,1792]{1,0:T(8,128)(2,1)}) %all-gather.3.cloned.1.call-update) | async-done | bytes 14680080 | tf_op jit(solution)/shard_map/all_gather | solution.py:25
  196.5 0.0 copy-done.1
  196.5 0.0 copy-done.2
  196.5 15.1 %fusion.9 = (bf16[480,1792]{1,0:T(8,128)(2,1)}, bf16[480,1792]{1,0:T(8,128)(2,1)}) fusion(bf16[480,1792]{1,0:T(8,128)(2,1)S(1)} %copy-done.1, bf16[480,1792]{1,0:T(8,128)(2,1)S(1)} %copy-done.2, bf16[480,4096]{1,0:T(8,128)(2,1)} %all-gather.5.cloned.1.call-done, bf16[4096,1792]{1,0:T(8,128)(2,1)} %all-gather.3.cloned.1.call-done), kind=kOutput, calls=%fused_computation.16 | convolution fusion | flops 7059333120 | bytes 25493504 | tf_op jit(solution)/shard_map/dot_general | solution.py:23
  211.6 166.2 %reduce-scatter.4.cloned.1.call-done = bf16[128,1792]{1,0:T(8,128)(2,1)} async-done(((bf16[4096,1792]{1,0:T(8,128)(2,1)}), bf16[128,1792]{1,0:T(8,128)(2,1)}) %reduce-scatter.4.cloned.1.call-update) | async-done | bytes 458768
  377.9 1.3 copy.11
  379.1 1.1 copy.9
Async XLA Ops:
  7.2 0.8 copy-start
  7.2 59.1 %all-gather.5.cloned.1.call-start = ((), (), s32[]{:S(2)}) async-start(), calls=%async_computation.2 | async-start | bytes 4423680 | tf_op jit(solution)/shard_map/all_gather | solution.py:15
  7.9 188.6 %all-gather.3.cloned.1.call-start = ((), (), s32[]{:S(2)}) async-start(), calls=%async_computation.1 | async-start | bytes 15138816 | tf_op jit(solution)/shard_map/all_gather | solution.py:25
  9.9 367.9 %reduce-scatter.4.cloned.1.call-start = ((), (), s32[]{:S(2)}) async-start(), calls=%async_computation.3 | async-start | bytes 15138816
  99.1 97.4 %copy-start.1 = (bf16[480,1792]{1,0:T(8,128)(2,1)S(1)}, bf16[480,1792]{1,0:T(8,128)(2,1)}, u32[]{:S(2)}) copy-start(bf16[480,1792]{1,0:T(8,128)(2,1)} %param.6) | copy-start | bytes 5160964
  99.1 97.4 %copy-start.2 = (bf16[480,1792]{1,0:T(8,128)(2,1)S(1)}, bf16[480,1792]{1,0:T(8,128)(2,1)}, u32[]{:S(2)}) copy-start(bf16[480,1792]{1,0:T(8,128)(2,1)} %param.7) | copy-start | bytes 5160964
Sparse Core Ops, SparseCore 0:
  9.8 56.4 all-gather.4
  69.6 126.8 all-gather.2
  201.1 176.7 reduce-scatter.3
where the time goes:
time: 390 us; the launch traced here: 387 us
  waiting for transfers between devices  321 us (82%)
  matrix products  29.1 us (7%)
  local copies, waits for them, and re-layouts  21.3 us (5%)
  between operations  13.8 us (4%)
    unnamed x4, waiting for transfers between devices  167 us
    all_gather x1, waiting for transfers between devices, per_device(): lax.all_gather(weight, 'node', axis=0, tiled=True)  97.4 us
    all_gather x1, waiting for transfers between devices, per_device(): full_grad = lax.all_gather(out_grad, 'local', axis=1, tiled=True)  56.3 us
    unnamed x9, local copies, waits for them, and re-layouts  21.3 us
    dot_general x1, matrix products, per_device(): jnp.dot(columns, lax.all_gather(weight, 'node', axis=0, tiled=True), pref...  15.1 us
    dot_general x1, matrix products, per_device(): lax.dot_general(columns, hidden, (((0,), (0,)), ((), ())), preferred_elem...  14 us
  transfers between devices with their start and end apart: 3, of which 3 were waited for; matrix products, arithmetic and copies ran while one was open for 13% of the time, Pallas kernels for 0%

commit v1 on v0

v1 whole, which is shorter than its diff:
```python
import jax
import jax.numpy as jnp
from jax import lax
from jax.experimental import pallas as pl
from jax.experimental.pallas import tpu as pltpu
from jax.sharding import Mesh, PartitionSpec as P

AXES = ("z", "yh", "c", "yl", "x")
SIZES = (8, 2, 2, 2, 4)
BF = jnp.bfloat16
F32 = jnp.float32
TOK = 480
SIDE = 128
TILE = 256
EARLY = 256
FIRST, REST = 1024, 768
SWAP = [(0, 1), (1, 0)]
PARAMS = pltpu.CompilerParams(vmem_limit_bytes=60 * 1024 * 1024)
ANY = pl.BlockSpec(memory_space=pl.ANY)
TOKEN = pl.BlockSpec(memory_space=pltpu.SMEM)
TOKEN_TYPE = jax.ShapeDtypeStruct((8,), jnp.int32)


def cost(flops, size):
    return pl.CostEstimate(flops=flops, bytes_accessed=size, transcendentals=0)


def dequantize(tiles, scales):
    rows, cols = tiles.shape
    side = rows // scales.shape[0]
    blocks = tiles.astype(F32).reshape(rows // side, side, cols // side, side)
    return (blocks * scales[:, None, :, None]).reshape(rows, cols).astype(BF)


def shift(value, axis, size, by):
    return lax.ppermute(value, axis, [(i, (i + by) % size) for i in range(size)])


def pass_token(places, order):
    for i in range(8):
        order[i] = places[i]


def down_kernel(places, *refs):
    grads, early, late = refs[:8], refs[8:12], refs[12:16]
    out, order, raw, turned, tall, ready, loaded, arrived, left = refs[16:]
    loads = [pltpu.make_async_copy(grads[i], raw.at[i], loaded.at[i]) for i in range(8)]
    cols = tall.shape[1]
    wide = [
        pltpu.make_async_copy(
            part[r], tall.at[pl.ds(r * TOK, TOK), pl.ds(at, size)], arrived.at[k, r]
        )
        for k, (part, at, size) in enumerate(((early, 0, EARLY), (late, EARLY, cols - EARLY)))
        for r in range(4)
    ]
    for copy in loads + wide:
        copy.start()
    for i in range(8):
        loads[i].wait()
        at = pl.multiple_of(places[i] * SIDE, SIDE)
        turned[pl.ds(at, SIDE), :] = raw[i].T
    pass_token(places, order)
    for copy in wide:
        copy.wait()
    stores = []
    for n in range(cols // TILE):
        at = pl.ds(n * TILE, TILE)
        ready[:, at] = jnp.dot(turned[...], tall[:, at], preferred_element_type=F32).astype(BF)
        stores.append(pltpu.make_async_copy(ready.at[:, at], out.at[:, at], left.at[n]))
        stores[n].start()
    for copy in stores:
        copy.wait()


def down_partial(places, grads, early, late):
    cols = early[0].shape[1] + late[0].shape[1]
    return pl.pallas_call(
        down_kernel,
        out_shape=(jax.ShapeDtypeStruct((8 * SIDE, cols), BF), TOKEN_TYPE),
        in_specs=[TOKEN] + [ANY] * 16,
        out_specs=(ANY, TOKEN),
        scratch_shapes=[
            pltpu.VMEM((8, 4 * TOK, SIDE), BF),
            pltpu.VMEM((8 * SIDE, 4 * TOK), BF),
            pltpu.VMEM((4 * TOK, cols), BF),
            pltpu.VMEM((8 * SIDE, cols), BF),
            pltpu.SemaphoreType.DMA((8,)),
            pltpu.SemaphoreType.DMA((2, 4)),
            pltpu.SemaphoreType.DMA((cols // TILE,)),
        ],
        compiler_params=PARAMS,
        cost_estimate=cost(2 * 8 * SIDE * 4 * TOK * cols, 14 << 20),
        name="down_partial",
    )(places, *grads, *early, *late)


def up_kernel(places, *refs):
    grads, weights, send, keep, pass_on, order, joined, sems = refs[:8], *refs[8:]

    @pl.when(pl.program_id(0) == 0)
    def _():
        loads = []
        for i in range(8):
            at = pl.ds(pl.multiple_of(places[i] * SIDE, SIDE), SIDE)
            loads.append(pltpu.make_async_copy(grads[i], joined.at[:, at], sems.at[i]))
            loads[i].start()
        pass_token(places, order)
        for copy in loads:
            copy.wait()

    w = weights[...]
    for r in range(4):
        rows = joined[r * TOK : (r + 1) * TOK, :]
        part = jnp.dot(rows, w, preferred_element_type=F32)
        if r % 2:
            send[r // 2] = part.astype(BF)
        elif r == 0:
            keep[...] = part
        else:
            pass_on[...] = part


def hidden_partial(places, grads, weights, start, cols):
    first = start // TILE
    one = pl.BlockSpec((TOK, TILE), lambda n: (0, n))
    return pl.pallas_call(
        up_kernel,
        out_shape=(
            jax.ShapeDtypeStruct((2, TOK, cols), BF),
            jax.ShapeDtypeStruct((TOK, cols), F32),
            jax.ShapeDtypeStruct((TOK, cols), F32),
            TOKEN_TYPE,
        ),
        grid=(cols // TILE,),
        in_specs=[TOKEN]
        + [ANY] * 8
        + [pl.BlockSpec((8 * SIDE, TILE), lambda n: (0, n + first))],
        out_specs=(pl.BlockSpec((2, TOK, TILE), lambda n: (0, 0, n)), one, one, TOKEN),
        scratch_shapes=[
            pltpu.VMEM((4 * TOK, 8 * SIDE), BF),
            pltpu.SemaphoreType.DMA((8,)),
        ],
        compiler_params=PARAMS,
        cost_estimate=cost(2 * 8 * SIDE * 4 * TOK * cols, 10 << 20),
        name="hidden_partial",
    )(places, *grads, weights)


def add_kernel(places, own, came, out, order):
    out[...] = (own[...] + came[...].astype(F32)).astype(BF)
    pass_token(places, order)


def add_partner(places, own, came):
    cols = own.shape[1]
    one = pl.BlockSpec((TOK, cols), lambda n: (0, 0))
    return pl.pallas_call(
        add_kernel,
        out_shape=(jax.ShapeDtypeStruct((TOK, cols), BF), TOKEN_TYPE),
        grid=(1,),
        in_specs=[TOKEN, one, pl.BlockSpec((None, TOK, cols), lambda n: (1, 0, 0))],
        out_specs=(one, TOKEN),
        compiler_params=PARAMS,
        cost_estimate=cost(TOK * cols, 8 * TOK * cols),
        name="add_partner",
    )(places, own, came)


def finish_kernel(gate_pre, up_pre, keep, came, far, *refs):
    gate_out, up_out = refs[-2:]
    hidden_grad = keep[...] + came[...].astype(F32) + far[...].astype(F32)
    gate = gate_pre[...].astype(F32)
    up = up_pre[...].astype(F32)
    sig = 0.5 + 0.5 * jnp.tanh(0.5 * gate)
    swish = gate * sig
    gate_out[...] = (hidden_grad * up * (sig + swish * (1.0 - sig))).astype(BF)
    up_out[...] = (hidden_grad * swish).astype(BF)


def finish(gate_pre, up_pre, keep, came, far, start, cols, made):
    first = start // TILE
    wide = pl.BlockSpec((TOK, TILE), lambda n: (0, n + first))
    one = pl.BlockSpec((TOK, TILE), lambda n: (0, n))
    half = pl.BlockSpec((None, TOK, TILE), lambda n: (0, 0, n))
    return pl.pallas_call(
        finish_kernel,
        out_shape=(jax.ShapeDtypeStruct(gate_pre.shape, BF),) * 2,
        grid=(cols // TILE,),
        in_specs=[wide, wide, one, half, one] + [ANY] * len(made),
        out_specs=(wide, wide),
        input_output_aliases={5 + i: i for i in range(len(made))},
        compiler_params=PARAMS,
        cost_estimate=cost(20 * TOK * cols, 16 * TOK * cols),
        name="finish",
    )(gate_pre, up_pre, keep, came, far, *made)


def per_device(out_grad, gate_pre, up_pre, down_tiles, down_scales):
    yh, c = lax.axis_index("yh"), lax.axis_index("c")
    yl, x = lax.axis_index("yl"), lax.axis_index("x")

    def block(r):
        other = 2 * (yh ^ (r >> 1)) + (c ^ (r & 1))
        return lax.dynamic_slice(out_grad, (0, other * SIDE), (TOK, SIDE))

    gate = gate_pre.astype(F32)
    h0 = (gate * jax.nn.sigmoid(gate) * up_pre.astype(F32)).astype(BF)
    ha, hb = h0[:, :EARLY], h0[:, EARLY:]
    near, ha = lax.optimization_barrier((lax.ppermute(block(1), "c", SWAP), ha))
    pieces = (
        block(0),
        near,
        lax.ppermute(block(2), "yh", SWAP),
        lax.ppermute(block(3), ("yh", "c"), [(i, 3 - i) for i in range(4)]),
    )
    ha2 = lax.ppermute(ha, "yh", SWAP)
    ha1 = lax.ppermute(ha, "c", SWAP)
    *pieces, ha1 = lax.optimization_barrier((*pieces, ha1))
    g = jnp.concatenate(pieces, axis=0)

    weight = dequantize(down_tiles, down_scales)
    weights = lax.all_gather(weight, "z", axis=0, tiled=True)

    gy = lax.ppermute(g, "yl", SWAP)
    g_m, g_p = shift(g, "x", 4, 1), shift(g, "x", 4, -1)
    gy, g_m, g_p, hb, ha2 = lax.optimization_barrier((gy, g_m, g_p, hb, ha2))
    gy_m, gy_p = shift(gy, "x", 4, 1), shift(gy, "x", 4, -1)
    g_far = shift(g_m, "x", 4, 1)
    hb2 = lax.ppermute(hb, "yh", SWAP)
    hb1, ha3 = lax.ppermute(hb, "c", SWAP), lax.ppermute(ha2, "c", SWAP)
    gy_far = shift(gy_p, "x", 4, -1)
    hb2, gy_m, g_far, gy_far, ha3, hb1 = lax.optimization_barrier(
        (hb2, gy_m, g_far, gy_far, ha3, hb1)
    )
    hb3 = lax.ppermute(hb2, "c", SWAP)

    grads = (g, gy, g_m, g_p, gy_m, gy_p, g_far, gy_far)
    places = jnp.stack(
        [
            (yl ^ dy) * 4 + ((x + dx) & 3)
            for dy, dx in ((0, 0), (1, 0), (0, 3), (0, 1), (1, 3), (1, 1), (0, 2), (1, 2))
        ]
    ).astype(jnp.int32)

    down, places = down_partial(places, grads, (ha, ha1, ha2, ha3), (hb, hb1, hb2, hb3))
    total = lax.psum_scatter(down, "z", scatter_dimension=0, tiled=True).astype(F32)

    send, keep_a, pass_on, places = hidden_partial(places, grads, weights, 0, FIRST)
    came_a = lax.ppermute(send, "c", SWAP)
    chip, places = add_partner(places, pass_on, came_a)
    far_a = lax.ppermute(chip, "yh", SWAP)

    send, keep_b, pass_on, places = hidden_partial(places, grads, weights, FIRST, REST)
    came_b = lax.ppermute(send, "c", SWAP)
    chip, places = add_partner(places, pass_on, came_b)
    far_b = lax.ppermute(chip, "yh", SWAP)

    made = finish(gate_pre, up_pre, keep_a, came_a, far_a, 0, FIRST, ())
    made = finish(gate_pre, up_pre, keep_b, came_b, far_b, FIRST, REST, made)
    return (*made, total)


def solution(mesh):
    fine = Mesh(mesh.devices.reshape(SIZES), AXES)
    spec = P(("z", "yh", "c"), ("yl", "x"))
    return jax.shard_map(
        per_device,
        mesh=fine,
        in_specs=(spec,) * 5,
        out_specs=(spec,) * 3,
        check_vma=False,
    )
```

time: 390 us -> 184 us (0.47)
  waiting for transfers between devices: 321 us -> 86.3 us
  Pallas kernels: 0 us -> 47.1 us
  matrix products: 29.1 us -> 0 us
  starting transfers between devices: 0.12 us -> 23.6 us
  local copies, waits for them, and re-layouts: 21.3 us -> 5.94 us
  other arithmetic: 1.86 us -> 6.38 us
    unnamed x4 -> x2, waiting for transfers between devices: 167 us -> 0.03 us
    all_gather x2 -> x1, waiting for transfers between devices: 154 us -> 0.02 us  [per_device(): weights = lax.all_gather(weight, 'z', axis=0, tiled=True)]
    ppermute x0 -> x20, waiting for transfers between devices: none -> 86.2 us  [the longest x6 19.9 us: shift(): lax.ppermute(value, axis, [(i, (i + by) % size) for i in range(size)])]
    pallas_call x0 -> x7, Pallas kernels: none -> 47.1 us  [the longest x2 17.6 us: hidden_partial(): pl.pallas_call(up_kernel, out_shape=(jax.ShapeDtypeStruct((2, TOK, cols),...]
    dot_general x2 -> x0, matrix products: 29.1 us -> none  [the longest x1 15.1 us: per_device(): jnp.dot(columns, lax.all_gather(weight, 'node', axis=0, tiled=True), pref...]
    ppermute x0 -> x20, starting transfers between devices: none -> 23.5 us  [the longest x6 7.74 us: shift(): lax.ppermute(value, axis, [(i, (i + by) % size) for i in range(size)])]
    unnamed x9 -> x45, local copies, waits for them, and re-layouts: 21.3 us -> 4.97 us
    convert_element_type x1 -> x3, other arithmetic: 1.86 us -> 6.38 us  [the longest x1 2.51 us: per_device(): h0 = (gate * jax.nn.sigmoid(gate) * up_pre.astype(F32)).astype(BF)]
  transfers between devices with their start and end apart: 3 -> 22, of which waited for: 3 -> 12; matrix products, arithmetic and copies ran while one was open for 13% -> 2% of each run, Pallas kernels for 0% -> 26%
where the time goes in v1:
time: 184 us
  waiting for transfers between devices  86.3 us (47%)
  Pallas kernels  47.1 us (26%)
  starting transfers between devices  23.6 us (13%)
  between operations  14.4 us (8%)
  other arithmetic  6.38 us (3%)
  local copies, waits for them, and re-layouts  5.94 us (3%)
    ppermute x6, waiting for transfers between devices, shift(): lax.ppermute(value, axis, [(i, (i + by) % size) for i in range(size)])  19.9 us
    pallas_call x2, Pallas kernels, hidden_partial(): pl.pallas_call(up_kernel, out_shape=(jax.ShapeDtypeStruct((2, TOK, cols),...  17.6 us
    ppermute x1, waiting for transfers between devices, per_device(): far_a = lax.ppermute(chip, 'yh', SWAP)  17.4 us
    ppermute x1, waiting for transfers between devices, per_device(): ha2 = lax.ppermute(ha, 'yh', SWAP)  15.4 us
    pallas_call x1, Pallas kernels, down_partial(): pl.pallas_call(down_kernel, out_shape=(jax.ShapeDtypeStruct((8 * SIDE, co...  14.4 us
    ppermute x1, waiting for transfers between devices, per_device(): far_b = lax.ppermute(chip, 'yh', SWAP)  9.76 us
    pallas_call x2, Pallas kernels, finish(): pl.pallas_call(finish_kernel, out_shape=(jax.ShapeDtypeStruct(gate_pre.sh...  9.63 us
    ppermute x6, starting transfers between devices, shift(): lax.ppermute(value, axis, [(i, (i + by) % size) for i in range(size)])  7.74 us
  transfers between devices with their start and end apart: 22, of which 12 were waited for; matrix products, arithmetic and copies ran while one was open for 2% of the time, Pallas kernels for 26%

profile of v1, /device:TPU:1, one launch (start us, length us, event | category | flops | bytes accessed | tf_op | source)
XLA Modules:
  0.0 183.7 jit_solution(9267534984446416581)
XLA Ops:
  10.0 3.3 %collective-permute-start = (bf16[480,128]{1,0:T(8,128)(2,1)S(1)}, bf16[480,128]{1,0:T(8,128)(2,1)S(1)}, u32[]{:S(2)}, u32[]{:S(2)}) collective-permute-start(bf16[480,128]{1,0:T(8,128)(2,1)S(1)} %get-tuple-element.74), channel_id=1, source_target_pairs={{0,8},{8,0},{1,9},{9,1},{2,10},{10,2},{3,11},{11,3},{4,12},{12,4},... | collective-permute-start | bytes 368648 | tf_op jit(solution)/shard_map/ppermute | solution.py:209
  13.3 2.5 %fusion.4 = bf16[480,1792]{1,0:T(8,128)(2,1)S(1)} fusion(bf16[480,1792]{1,0:T(8,128)(2,1)} %up_pre.3, bf16[480,1792]{1,0:T(8,128)(2,1)S(1)} %copy-done.1), kind=kLoop, calls=%fused_computation.6 | loop fusion | flops 6881280 | bytes 5160960 | tf_op jit(solution)/shard_map/convert_element_type | solution.py:207
  19.3 3.8 %collective-permute-done.2 = bf16[480,128]{1,0:T(8,128)(2,1)S(1)} collective-permute-done((bf16[480,128]{1,0:T(8,128)(2,1)S(1)}, bf16[480,128]{1,0:T(8,128)(2,1)S(1)}, u32[]{:S(2)}, u32[]{:S(2)}) %collective-permute-start.2) | collective-permute-done | bytes 122912 | tf_op jit(solution)/shard_map/ppermute | solution.py:214
  23.2 2.4 %collective-permute-done.1 = bf16[480,128]{1,0:T(8,128)(2,1)S(1)} collective-permute-done((bf16[480,128]{1,0:T(8,128)(2,1)S(1)}, bf16[480,128]{1,0:T(8,128)(2,1)S(1)}, u32[]{:S(2)}, u32[]{:S(2)}) %collective-permute-start.1) | collective-permute-done | bytes 122912 | tf_op jit(solution)/shard_map/ppermute | solution.py:213
  27.8 2.6 %collective-permute-start.7 = (bf16[480,256]{1,0:T(8,128)(2,1)S(1)}, bf16[480,256]{1,0:T(8,128)(2,1)S(1)}, u32[]{:S(2)}, u32[]{:S(2)}) collective-permute-start(bf16[480,256]{1,0:T(8,128)(2,1)S(1)} %slice.8.refs_8_), channel_id=1, source_target_pairs={{0,16},{16,0},{1,17},{17,1},{2,18},{18,2},{3,19},{19,3},{4,20},{20... | collective-permute-start | bytes 737288 | tf_op jit(solution)/shard_map/ppermute | solution.py:216
  30.5 15.4 %collective-permute-done.7.refs_10_ = bf16[480,256]{1,0:T(8,128)(2,1)S(1)} collective-permute-done((bf16[480,256]{1,0:T(8,128)(2,1)S(1)}, bf16[480,256]{1,0:T(8,128)(2,1)S(1)}, u32[]{:S(2)}, u32[]{:S(2)}) %collective-permute-start.7) | collective-permute-done | bytes 245792 | tf_op jit(solution)/shard_map/ppermute | solution.py:216
  48.3 2.7 %collective-permute-start.11 = (bf16[1920,128]{1,0:T(8,128)(2,1)S(1)}, bf16[1920,128]{1,0:T(8,128)(2,1)S(1)}, u32[]{:S(2)}, u32[]{:S(2)}) collective-permute-start(bf16[1920,128]{1,0:T(8,128)(2,1)S(1)} %collective-permute-done.4.refs_1_), channel_id=1, source_target_pairs={{0,3},{1,0},{2,1},{3,2},{4,7},{5,4},{6,5},{7,6},{8,11},{9,8},{10,9... | collective-permute-start | bytes 1474568 | tf_op jit(solution)/shard_map/ppermute | solution.py:36
  52.9 8.3 %collective-permute-done.11.refs_5_ = bf16[1920,128]{1,0:T(8,128)(2,1)S(1)} collective-permute-done((bf16[1920,128]{1,0:T(8,128)(2,1)S(1)}, bf16[1920,128]{1,0:T(8,128)(2,1)S(1)}, u32[]{:S(2)}, u32[]{:S(2)}) %collective-permute-start.11) | collective-permute-done | bytes 491552 | tf_op jit(solution)/shard_map/ppermute | solution.py:36
  61.3 3.5 %collective-permute-start.12 = (bf16[1920,128]{1,0:T(8,128)(2,1)S(1)}, bf16[1920,128]{1,0:T(8,128)(2,1)S(1)}, u32[]{:S(2)}, u32[]{:S(2)}) collective-permute-start(bf16[1920,128]{1,0:T(8,128)(2,1)S(1)} %collective-permute-done.11.refs_5_), channel_id=1, source_target_pairs={{0,3},{1,0},{2,1},{3,2},{4,7},{5,4},{6,5},{7,6},{8,11},{9,8},{10,9... | collective-permute-start | bytes 1474568 | tf_op jit(solution)/shard_map/ppermute | solution.py:36
  64.8 11.6 %collective-permute-done.10.refs_6_ = bf16[1920,128]{1,0:T(8,128)(2,1)S(1)} collective-permute-done((bf16[1920,128]{1,0:T(8,128)(2,1)S(1)}, bf16[1920,128]{1,0:T(8,128)(2,1)S(1)}, u32[]{:S(2)}, u32[]{:S(2)}) %collective-permute-start.10) | collective-permute-done | bytes 491552 | tf_op jit(solution)/shard_map/ppermute | solution.py:36
  76.4 7.0 %collective-permute-done.8.refs_14_ = bf16[480,1536]{1,0:T(8,128)(2,1)} collective-permute-done((bf16[480,1536]{1,0:T(8,128)(2,1)S(1)}, bf16[480,1536]{1,0:T(8,128)(2,1)}, u32[]{:S(2)}, u32[]{:S(2)}) %collective-permute-start.8) | collective-permute-done | bytes 1474592 | tf_op jit(solution)/shard_map/ppermute | solution.py:229
  85.3 2.6 %collective-permute-done.15.refs_15_ = bf16[480,1536]{1,0:T(8,128)(2,1)} collective-permute-done((bf16[480,1536]{1,0:T(8,128)(2,1)}, bf16[480,1536]{1,0:T(8,128)(2,1)}, u32[]{:S(2)}, u32[]{:S(2)}) %collective-permute-start.15) | collective-permute-done | bytes 1474592 | tf_op jit(solution)/shard_map/ppermute | solution.py:235
  87.9 14.4 %down_partial.1 = (bf16[1024,1792]{1,0:T(8,128)(2,1)}, s32[8]{0:T(128)}) custom-call(s32[8]{0:T(128)} %stack.35.places, bf16[1920,128]{1,0:T(8,128)(2,1)} %copy-done.9, bf16[1920,128]{1,0:T(8,128)(2,1)} %copy-done.14, bf16[1920,128]{1,0:T(8,128)(2,1)} %copy-done.13, bf16[1920,128]{1,0:T(8,128)(2,1)} %copy-done.12, bf16[1920,128]{1,0:T(8,128)(2,1)} %copy-done.16, ...), custom_call_target="tpu_custom_call" | custom-call | flops 7046430720 | bytes 14680064 | tf_op jit(solution)/shard_map/down_partial/pallas_call | solution.py:77
  102.3 9.4 %hidden_partial.2 = (bf16[2,480,1024]{2,1,0:T(8,128)(2,1)}, f32[480,1024]{1,0:T(8,128)}, f32[480,1024]{1,0:T(8,128)}, s32[8]{0:T(128)}) custom-call(s32[8]{0:T(128)} %get-tuple-element.56.places, bf16[1920,128]{1,0:T(8,128)(2,1)} %copy-done.9, bf16[1920,128]{1,0:T(8,128)(2,1)} %copy-done.14, bf16[1920,128]{1,0:T(8,128)(2,1)} %copy-done.13, ...), custom_call_target="tpu_custom_call" | custom-call | flops 4026531840 | bytes 10485760 | tf_op jit(solution)/shard_map/hidden_partial/pallas_call | solution.py:126
  112.2 3.8 %collective-permute-done.16.came = bf16[2,480,1024]{2,1,0:T(8,128)(2,1)S(1)} collective-permute-done((bf16[2,480,1024]{2,1,0:T(8,128)(2,1)}, bf16[2,480,1024]{2,1,0:T(8,128)(2,1)S(1)}, u32[]{:S(2)}, u32[]{:S(2)}) %collective-permute-start.16) | collective-permute-done | bytes 1966112 | tf_op jit(solution)/shard_map/ppermute | solution.py:249
  117.3 2.9 %add_partner.2 = (bf16[480,1024]{1,0:T(8,128)(2,1)}, s32[8]{0:T(128)}) custom-call(s32[8]{0:T(128)} %get-tuple-element.57.places, f32[480,1024]{1,0:T(8,128)} %get-tuple-element.58.own, bf16[2,480,1024]{2,1,0:T(8,128)(2,1)} %copy-done.2), custom_call_target="tpu_custom_call" | custom-call | flops 491520 | bytes 3932160 | tf_op jit(solution)/shard_map/add_partner/pallas_call | solution.py:157
  120.3 8.2 %hidden_partial.3 = (bf16[2,480,768]{2,1,0:T(8,128)(2,1)}, f32[480,768]{1,0:T(8,128)}, f32[480,768]{1,0:T(8,128)}, s32[8]{0:T(128)}) custom-call(s32[8]{0:T(128)} %get-tuple-element.60.places, bf16[1920,128]{1,0:T(8,128)(2,1)} %copy-done.9, bf16[1920,128]{1,0:T(8,128)(2,1)} %copy-done.14, bf16[1920,128]{1,0:T(8,128)(2,1)} %copy-done.13, ...), custom_call_target="tpu_custom_call" | custom-call | flops 3019898880 | bytes 10485760 | tf_op jit(solution)/shard_map/hidden_partial/pallas_call | solution.py:126
  129.2 2.8 %collective-permute-done.17.came = bf16[2,480,768]{2,1,0:T(8,128)(2,1)S(1)} collective-permute-done((bf16[2,480,768]{2,1,0:T(8,128)(2,1)}, bf16[2,480,768]{2,1,0:T(8,128)(2,1)S(1)}, u32[]{:S(2)}, u32[]{:S(2)}) %collective-permute-start.17) | collective-permute-done | bytes 1474592 | tf_op jit(solution)/shard_map/ppermute | solution.py:254
  133.2 2.6 %add_partner.3 = (bf16[480,768]{1,0:T(8,128)(2,1)}, s32[8]{0:T(128)}) custom-call(s32[8]{0:T(128)} %get-tuple-element.63.places, f32[480,768]{1,0:T(8,128)} %get-tuple-element.64.own, bf16[2,480,768]{2,1,0:T(8,128)(2,1)} %copy-done.3), custom_call_target="tpu_custom_call" | custom-call | flops 368640 | bytes 2949120 | tf_op jit(solution)/shard_map/add_partner/pallas_call | solution.py:157
  136.2 17.4 %collective-permute-done.19.far = bf16[480,1024]{1,0:T(8,128)(2,1)S(1)} collective-permute-done((bf16[480,1024]{1,0:T(8,128)(2,1)S(1)}, bf16[480,1024]{1,0:T(8,128)(2,1)S(1)}, u32[]{:S(2)}, u32[]{:S(2)}) %collective-permute-start.19) | collective-permute-done | bytes 983072 | tf_op jit(solution)/shard_map/ppermute | solution.py:251
  154.6 5.1 %finish.2 = (bf16[480,1792]{1,0:T(8,128)(2,1)}, bf16[480,1792]{1,0:T(8,128)(2,1)}) custom-call(bf16[480,1792]{1,0:T(8,128)(2,1)} %gate_pre.3, bf16[480,1792]{1,0:T(8,128)(2,1)} %up_pre.3, f32[480,1024]{1,0:T(8,128)} %get-tuple-element.66.keep, bf16[2,480,1024]{2,1,0:T(8,128)(2,1)} %copy-done.2, bf16[480,1024]{1,0:T(8,128)(2,1)} %copy-done.5), custom_call_target="tpu_custom_call" | custom-call | flops 9830400 | bytes 7864320 | tf_op jit(solution)/shard_map/finish/pallas_call | solution.py:185
  159.7 9.8 %collective-permute-done.18.far = bf16[480,768]{1,0:T(8,128)(2,1)S(1)} collective-permute-done((bf16[480,768]{1,0:T(8,128)(2,1)}, bf16[480,768]{1,0:T(8,128)(2,1)S(1)}, u32[]{:S(2)}, u32[]{:S(2)}) %collective-permute-start.18) | collective-permute-done | bytes 737312 | tf_op jit(solution)/shard_map/ppermute | solution.py:256
  170.3 4.6 %finish.3 = (bf16[480,1792]{1,0:T(8,128)(2,1)}, bf16[480,1792]{1,0:T(8,128)(2,1)}) custom-call(bf16[480,1792]{1,0:T(8,128)(2,1)} %gate_pre.3, bf16[480,1792]{1,0:T(8,128)(2,1)} %up_pre.3, f32[480,768]{1,0:T(8,128)} %get-tuple-element.61.keep, bf16[2,480,768]{2,1,0:T(8,128)(2,1)} %copy-done.3, ...), custom_call_target="tpu_custom_call", output_to_operand_aliasing={{0}: (5, {}), {1}: (6, {})} | custom-call | flops 7372800 | bytes 5898240 | tf_op jit(solution)/shard_map/finish/pallas_call | solution.py:185
  174.8 2.0 %convert_element_type.23 = f32[128,1792]{1,0:T(8,128)} convert(bf16[128,1792]{1,0:T(8,128)(2,1)} %reduce-scatter.2.cloned.1.call-done) | non-fusion elementwise | flops 229376 | bytes 1376256 | tf_op jit(solution)/shard_map/convert_element_type | solution.py:246
  (83 shorter events, 20.6 us)
Async XLA Ops:
  7.2 95.1 %all-gather.2.cloned.1.call-start = ((), (), s32[]{:S(2)}) async-start(), calls=%async_computation.1 | async-start | bytes 4128768 | tf_op jit(solution)/shard_map/all_gather | solution.py:222
  9.8 165.0 %reduce-scatter.2.cloned.1.call-start = ((), (), s32[]{:S(2)}) async-start(), calls=%async_computation.2 | async-start | bytes 4128768 | tf_op jit(solution)/shard_map/reduce_scatter | solution.py:246
  10.0 5.9 %collective-permute-start = (bf16[480,128]{1,0:T(8,128)(2,1)S(1)}, bf16[480,128]{1,0:T(8,128)(2,1)S(1)}, u32[]{:S(2)}, u32[]{:S(2)}) collective-permute-start(bf16[480,128]{1,0:T(8,128)(2,1)S(1)} %get-tuple-element.74), channel_id=1, source_target_pairs={{0,8},{8,0},{1,9},{9,1},{2,10},{10,2},{3,11},{11,3},{4,12},{12,4},... | collective-permute-start | bytes 368648 | tf_op jit(solution)/shard_map/ppermute | solution.py:209
  15.9 9.7 %collective-permute-start.3 = (bf16[480,256]{1,0:T(8,128)(2,1)S(1)}, bf16[480,256]{1,0:T(8,128)(2,1)S(1)}, u32[]{:S(2)}, u32[]{:S(2)}) collective-permute-start(bf16[480,256]{1,0:T(8,128)(2,1)S(1)} %slice.8.refs_8_), channel_id=1, source_target_pairs={{0,8},{8,0},{1,9},{9,1},{2,10},{10,2},{3,11},{11,3},{4,12},{12,4},... | collective-permute-start | bytes 737288 | tf_op jit(solution)/shard_map/ppermute | solution.py:217
  16.0 7.2 %collective-permute-start.2 = (bf16[480,128]{1,0:T(8,128)(2,1)S(1)}, bf16[480,128]{1,0:T(8,128)(2,1)S(1)}, u32[]{:S(2)}, u32[]{:S(2)}) collective-permute-start(bf16[480,128]{1,0:T(8,128)(2,1)S(1)} %get-tuple-element.73), channel_id=1, source_target_pairs={{0,24},{8,16},{16,8},{24,0},{1,25},{9,17},{17,9},{25,1},{2,26},{10... | collective-permute-start | bytes 368648 | tf_op jit(solution)/shard_map/ppermute | solution.py:214
  17.5 8.0 %collective-permute-start.1 = (bf16[480,128]{1,0:T(8,128)(2,1)S(1)}, bf16[480,128]{1,0:T(8,128)(2,1)S(1)}, u32[]{:S(2)}, u32[]{:S(2)}) collective-permute-start(bf16[480,128]{1,0:T(8,128)(2,1)S(1)} %get-tuple-element.76), channel_id=1, source_target_pairs={{0,16},{16,0},{1,17},{17,1},{2,18},{18,2},{3,19},{19,3},{4,20},{20... | collective-permute-start | bytes 368648 | tf_op jit(solution)/shard_map/ppermute | solution.py:213
  25.7 62.2 %copy-start.9 = (bf16[1920,128]{1,0:T(8,128)(2,1)}, bf16[1920,128]{1,0:T(8,128)(2,1)S(1)}, u32[]{:S(2)}) copy-start(bf16[1920,128]{1,0:T(8,128)(2,1)S(1)} %constant_dynamic-update-slice_fusion.refs_0_) | copy-start | bytes 1474564
  25.7 20.3 %collective-permute-start.6 = (bf16[1920,128]{1,0:T(8,128)(2,1)S(1)}, bf16[1920,128]{1,0:T(8,128)(2,1)S(1)}, u32[]{:S(2)}, u32[]{:S(2)}) collective-permute-start(bf16[1920,128]{1,0:T(8,128)(2,1)S(1)} %constant_dynamic-update-slice_fusion.refs_0_), channel_id=1, source_target_pairs={{0,3},{1,0},{2,1},{3,2},{4,7},{5,4},{6,5},{7,6},{8,11},{9,8},{10,9... | collective-permute-start | bytes 1474568 | tf_op jit(solution)/shard_map/ppermute | solution.py:36
  26.6 19.4 %collective-permute-start.5 = (bf16[1920,128]{1,0:T(8,128)(2,1)S(1)}, bf16[1920,128]{1,0:T(8,128)(2,1)S(1)}, u32[]{:S(2)}, u32[]{:S(2)}) collective-permute-start(bf16[1920,128]{1,0:T(8,128)(2,1)S(1)} %constant_dynamic-update-slice_fusion.refs_0_), channel_id=1, source_target_pairs={{0,1},{1,2},{2,3},{3,0},{4,5},{5,6},{6,7},{7,4},{8,9},{9,10},{10,1... | collective-permute-start | bytes 1474568 | tf_op jit(solution)/shard_map/ppermute | solution.py:36
  27.2 18.8 %collective-permute-start.4 = (bf16[1920,128]{1,0:T(8,128)(2,1)S(1)}, bf16[1920,128]{1,0:T(8,128)(2,1)S(1)}, u32[]{:S(2)}, u32[]{:S(2)}) collective-permute-start(bf16[1920,128]{1,0:T(8,128)(2,1)S(1)} %constant_dynamic-update-slice_fusion.refs_0_), channel_id=1, source_target_pairs={{0,4},{4,0},{1,5},{5,1},{2,6},{6,2},{3,7},{7,3},{8,12},{12,8},{9,1... | collective-permute-start | bytes 1474568 | tf_op jit(solution)/shard_map/ppermute | solution.py:224
  27.8 18.2 %collective-permute-start.7 = (bf16[480,256]{1,0:T(8,128)(2,1)S(1)}, bf16[480,256]{1,0:T(8,128)(2,1)S(1)}, u32[]{:S(2)}, u32[]{:S(2)}) collective-permute-start(bf16[480,256]{1,0:T(8,128)(2,1)S(1)} %slice.8.refs_8_), channel_id=1, source_target_pairs={{0,16},{16,0},{1,17},{17,1},{2,18},{18,2},{3,19},{19,3},{4,20},{20... | collective-permute-start | bytes 737288 | tf_op jit(solution)/shard_map/ppermute | solution.py:216
  30.5 57.3 %copy-start.4 = (bf16[480,1536]{1,0:T(8,128)(2,1)}, bf16[480,1536]{1,0:T(8,128)(2,1)S(1)}, u32[]{:S(2)}) copy-start(bf16[480,1536]{1,0:T(8,128)(2,1)S(1)} %slice.9.refs_12_) | copy-start | bytes 4423684
  46.0 30.4 %collective-permute-start.14 = (bf16[480,1536]{1,0:T(8,128)(2,1)S(1)}, bf16[480,1536]{1,0:T(8,128)(2,1)S(1)}, u32[]{:S(2)}, u32[]{:S(2)}) collective-permute-start(bf16[480,1536]{1,0:T(8,128)(2,1)S(1)} %slice.9.refs_12_), channel_id=1, source_target_pairs={{0,8},{8,0},{1,9},{9,1},{2,10},{10,2},{3,11},{11,3},{4,12},{12,4},... | collective-permute-start | bytes 4423688 | tf_op jit(solution)/shard_map/ppermute | solution.py:230
  48.0 35.5 %collective-permute-start.8 = (bf16[480,1536]{1,0:T(8,128)(2,1)S(1)}, bf16[480,1536]{1,0:T(8,128)(2,1)}, u32[]{:S(2)}, u32[]{:S(2)}) collective-permute-start(bf16[480,1536]{1,0:T(8,128)(2,1)S(1)} %slice.9.refs_12_), channel_id=1, source_target_pairs={{0,16},{16,0},{1,17},{17,1},{2,18},{18,2},{3,19},{19,3},{4,20},{20... | collective-permute-start | bytes 4423688 | tf_op jit(solution)/shard_map/ppermute | solution.py:229
  48.3 12.9 %collective-permute-start.11 = (bf16[1920,128]{1,0:T(8,128)(2,1)S(1)}, bf16[1920,128]{1,0:T(8,128)(2,1)S(1)}, u32[]{:S(2)}, u32[]{:S(2)}) collective-permute-start(bf16[1920,128]{1,0:T(8,128)(2,1)S(1)} %collective-permute-done.4.refs_1_), channel_id=1, source_target_pairs={{0,3},{1,0},{2,1},{3,2},{4,7},{5,4},{6,5},{7,6},{8,11},{9,8},{10,9... | collective-permute-start | bytes 1474568 | tf_op jit(solution)/shard_map/ppermute | solution.py:36
  51.0 1.9 %collective-permute-start.13 = (bf16[480,256]{1,0:T(8,128)(2,1)S(1)}, bf16[480,256]{1,0:T(8,128)(2,1)}, u32[]{:S(2)}, u32[]{:S(2)}) collective-permute-start(bf16[480,256]{1,0:T(8,128)(2,1)S(1)} %collective-permute-done.7.refs_10_), channel_id=1, source_target_pairs={{0,8},{8,0},{1,9},{9,1},{2,10},{10,2},{3,11},{11,3},{4,12},{12,4},... | collective-permute-start | bytes 737288 | tf_op jit(solution)/shard_map/ppermute | solution.py:230
  51.7 24.7 %collective-permute-start.9 = (bf16[1920,128]{1,0:T(8,128)(2,1)S(1)}, bf16[1920,128]{1,0:T(8,128)(2,1)S(1)}, u32[]{:S(2)}, u32[]{:S(2)}) collective-permute-start(bf16[1920,128]{1,0:T(8,128)(2,1)S(1)} %collective-permute-done.4.refs_1_), channel_id=1, source_target_pairs={{0,1},{1,2},{2,3},{3,0},{4,5},{5,6},{6,7},{7,4},{8,9},{9,10},{10,1... | collective-permute-start | bytes 1474568 | tf_op jit(solution)/shard_map/ppermute | solution.py:36
  52.9 23.4 %collective-permute-start.10 = (bf16[1920,128]{1,0:T(8,128)(2,1)S(1)}, bf16[1920,128]{1,0:T(8,128)(2,1)S(1)}, u32[]{:S(2)}, u32[]{:S(2)}) collective-permute-start(bf16[1920,128]{1,0:T(8,128)(2,1)S(1)} %collective-permute-done.5.refs_2_), channel_id=1, source_target_pairs={{0,1},{1,2},{2,3},{3,0},{4,5},{5,6},{6,7},{7,4},{8,9},{9,10},{10,1... | collective-permute-start | bytes 1474568 | tf_op jit(solution)/shard_map/ppermute | solution.py:36
  61.3 15.1 %collective-permute-start.12 = (bf16[1920,128]{1,0:T(8,128)(2,1)S(1)}, bf16[1920,128]{1,0:T(8,128)(2,1)S(1)}, u32[]{:S(2)}, u32[]{:S(2)}) collective-permute-start(bf16[1920,128]{1,0:T(8,128)(2,1)S(1)} %collective-permute-done.11.refs_5_), channel_id=1, source_target_pairs={{0,3},{1,0},{2,1},{3,2},{4,7},{5,4},{6,5},{7,6},{8,11},{9,8},{10,9... | collective-permute-start | bytes 1474568 | tf_op jit(solution)/shard_map/ppermute | solution.py:36
  83.5 4.4 %collective-permute-start.15 = (bf16[480,1536]{1,0:T(8,128)(2,1)}, bf16[480,1536]{1,0:T(8,128)(2,1)}, u32[]{:S(2)}, u32[]{:S(2)}) collective-permute-start(bf16[480,1536]{1,0:T(8,128)(2,1)} %collective-permute-done.8.refs_14_), channel_id=1, source_target_pairs={{0,8},{8,0},{1,9},{9,1},{2,10},{10,2},{3,11},{11,3},{4,12},{12,4},... | collective-permute-start | bytes 4423688 | tf_op jit(solution)/shard_map/ppermute | solution.py:235
  111.7 4.3 %collective-permute-start.16 = (bf16[2,480,1024]{2,1,0:T(8,128)(2,1)}, bf16[2,480,1024]{2,1,0:T(8,128)(2,1)S(1)}, u32[]{:S(2)}, u32[]{:S(2)}) collective-permute-start(bf16[2,480,1024]{2,1,0:T(8,128)(2,1)} %get-tuple-element.59), channel_id=1, source_target_pairs={{0,8},{8,0},{1,9},{9,1},{2,10},{10,2},{3,11},{11,3},{4,12},{12,4},... | collective-permute-start | bytes 5898248 | tf_op jit(solution)/shard_map/ppermute | solution.py:249
  128.4 3.6 %collective-permute-start.17 = (bf16[2,480,768]{2,1,0:T(8,128)(2,1)}, bf16[2,480,768]{2,1,0:T(8,128)(2,1)S(1)}, u32[]{:S(2)}, u32[]{:S(2)}) collective-permute-start(bf16[2,480,768]{2,1,0:T(8,128)(2,1)} %get-tuple-element.62), channel_id=1, source_target_pairs={{0,8},{8,0},{1,9},{9,1},{2,10},{10,2},{3,11},{11,3},{4,12},{12,4},... | collective-permute-start | bytes 4423688 | tf_op jit(solution)/shard_map/ppermute | solution.py:254
  128.9 24.7 %collective-permute-start.19 = (bf16[480,1024]{1,0:T(8,128)(2,1)S(1)}, bf16[480,1024]{1,0:T(8,128)(2,1)S(1)}, u32[]{:S(2)}, u32[]{:S(2)}) collective-permute-start(bf16[480,1024]{1,0:T(8,128)(2,1)S(1)} %copy-done.11), channel_id=1, source_target_pairs={{0,16},{16,0},{1,17},{17,1},{2,18},{18,2},{3,19},{19,3},{4,20},{20... | collective-permute-start | bytes 2949128 | tf_op jit(solution)/shard_map/ppermute | solution.py:251
  135.8 33.7 %collective-permute-start.18 = (bf16[480,768]{1,0:T(8,128)(2,1)}, bf16[480,768]{1,0:T(8,128)(2,1)S(1)}, u32[]{:S(2)}, u32[]{:S(2)}) collective-permute-start(bf16[480,768]{1,0:T(8,128)(2,1)} %get-tuple-element.65), channel_id=1, source_target_pairs={{0,16},{16,0},{1,17},{17,1},{2,18},{18,2},{3,19},{19,3},{4,20},{20... | collective-permute-start | bytes 2211848 | tf_op jit(solution)/shard_map/ppermute | solution.py:256
  (19 other events, 255.6 us)
Sparse Core Ops, SparseCore 0:
  9.9 53.6 all-gather.1
  102.4 50.4 reduce-scatter.1

commit v2 on v1

v2 whole, which is shorter than its diff:
```python
import functools

import jax
import jax.numpy as jnp
from jax import lax
from jax.experimental import pallas as pl
from jax.experimental.pallas import tpu as pltpu
from jax.sharding import Mesh, PartitionSpec as P

AXES = ("z", "yh", "c", "yl", "x")
SIZES = (8, 2, 2, 2, 4)
BF = jnp.bfloat16
F32 = jnp.float32
TOK = 480
SIDE = 128
TILE = 256
PARTS = (0, 512, 1024, 1792)
CUTS = (0, 768, 1536, 1792)
SWAP = [(0, 1), (1, 0)]
PARAMS = pltpu.CompilerParams(vmem_limit_bytes=60 * 1024 * 1024)
ANY = pl.BlockSpec(memory_space=pl.ANY)
TOKEN = pl.BlockSpec(memory_space=pltpu.SMEM)
TOKEN_TYPE = jax.ShapeDtypeStruct((8,), jnp.int32)


def cost(flops, size):
    return pl.CostEstimate(flops=flops, bytes_accessed=size, transcendentals=0)


def dequantize(tiles, scales):
    rows, cols = tiles.shape
    side = rows // scales.shape[0]
    blocks = tiles.astype(F32).reshape(rows // side, side, cols // side, side)
    return (blocks * scales[:, None, :, None]).reshape(rows, cols).astype(BF)


def shift(value, axis, size, by):
    return lax.ppermute(value, axis, [(i, (i + by) % size) for i in range(size)])


def pass_token(places, order):
    for i in range(8):
        order[i] = places[i]


def down_kernel(places, *refs):
    rows, hidden = refs[0], refs[1:13]
    out, order, turned, tall, ready, loaded, arrived, left = refs[13:]
    load = pltpu.make_async_copy(rows, turned, loaded)
    parts = [
        [
            pltpu.make_async_copy(
                hidden[4 * k + r],
                tall.at[pl.ds(r * TOK, TOK), pl.ds(PARTS[k], PARTS[k + 1] - PARTS[k])],
                arrived.at[k, r],
            )
            for r in range(4)
        ]
        for k in range(3)
    ]
    for copy in [load] + parts[0]:
        copy.start()
    pass_token(places, order)
    load.wait()
    for copy in parts[0]:
        copy.wait()
    for copy in parts[1] + parts[2]:
        copy.start()
    stores = []
    for n in range(tall.shape[1] // TILE):
        if n * TILE in PARTS[1:]:
            for copy in parts[PARTS.index(n * TILE)]:
                copy.wait()
        at = pl.ds(n * TILE, TILE)
        ready[:, at] = jnp.dot(turned[...], tall[:, at], preferred_element_type=F32).astype(BF)
        stores.append(pltpu.make_async_copy(ready.at[:, at], out.at[:, at], left.at[n]))
        stores[n].start()
    for copy in stores:
        copy.wait()


def down_partial(places, turned, hidden):
    cols = PARTS[-1]
    return pl.pallas_call(
        down_kernel,
        out_shape=(jax.ShapeDtypeStruct((8 * SIDE, cols), BF), TOKEN_TYPE),
        in_specs=[TOKEN] + [ANY] * 13,
        out_specs=(ANY, TOKEN),
        scratch_shapes=[
            pltpu.VMEM((8 * SIDE, 4 * TOK), BF),
            pltpu.VMEM((4 * TOK, cols), BF),
            pltpu.VMEM((8 * SIDE, cols), BF),
            pltpu.SemaphoreType.DMA,
            pltpu.SemaphoreType.DMA((3, 4)),
            pltpu.SemaphoreType.DMA((cols // TILE,)),
        ],
        compiler_params=PARAMS,
        cost_estimate=cost(1000, 1000),
        name="down_partial",
    )(places, turned, *hidden)


def up_kernel(spans, places, mine, their_own, their_far, weights, partner_weights, *refs):
    order, keep, *pass_on, joined, stacked, sems = refs
    n = pl.program_id(0)

    @pl.when(n == 0)
    def _():
        half = pl.ds(8 * SIDE, 8 * SIDE)
        targets = (
            joined.at[:, pl.ds(0, 8 * SIDE)],
            joined.at[pl.ds(0, TOK), half],
            joined.at[pl.ds(TOK, TOK), half],
        )
        loads = [
            pltpu.make_async_copy(source, target, sems.at[k])
            for k, (source, target) in enumerate(zip((mine, their_own, their_far), targets))
        ]
        for copy in loads:
            copy.start()
        pass_token(places, order)
        for copy in loads:
            copy.wait()

    stacked[: 8 * SIDE, :] = weights[...]
    stacked[8 * SIDE :, :] = partner_weights[...]
    part = jnp.dot(joined[...], stacked[...], preferred_element_type=F32)
    keep[...] = part[:TOK]
    other = part[TOK:].astype(BF)
    for (low, high), out in zip(spans, pass_on):

        @pl.when((n >= low) & (n < high))
        def _():
            out[...] = other


def hidden_partial(places, mine, theirs, weights, partner_weights, cuts):
    first, cols = cuts[0] // TILE, cuts[-1] - cuts[0]
    tiles = [(cut - cuts[0]) // TILE for cut in cuts]
    one = pl.BlockSpec((TOK, TILE), lambda n: (0, n))
    tile = pl.BlockSpec((8 * SIDE, TILE), lambda n: (0, n + first))

    def part(low, high):
        return pl.BlockSpec((TOK, TILE), lambda n: (0, jnp.clip(n - low, 0, high - low - 1)))

    spans = list(zip(tiles, tiles[1:]))
    return pl.pallas_call(
        functools.partial(up_kernel, spans),
        out_shape=(
            TOKEN_TYPE,
            jax.ShapeDtypeStruct((TOK, cols), F32),
            *(jax.ShapeDtypeStruct((TOK, (high - low) * TILE), BF) for low, high in spans),
        ),
        grid=(cols // TILE,),
        in_specs=[TOKEN, ANY, ANY, ANY, tile, tile],
        out_specs=(TOKEN, one, *(part(low, high) for low, high in spans)),
        scratch_shapes=[
            pltpu.VMEM((2 * TOK, 16 * SIDE), BF),
            pltpu.VMEM((16 * SIDE, TILE), BF),
            pltpu.SemaphoreType.DMA((3,)),
        ],
        compiler_params=PARAMS,
        cost_estimate=cost(1000, 1000),
        name="hidden_partial",
    )(places, mine, *theirs, weights, partner_weights)


def turn_kernel(places, *refs):
    grads, (turned, mine, send, send_far) = refs[:8], refs[8:]
    for i in range(8):
        at = pl.ds(pl.multiple_of(places[i] * SIDE, SIDE), SIDE)
        value = grads[i][...]
        turned[at, :] = value.T
        mine[:, at] = value[: 2 * TOK]
        send[:, at] = value[2 * TOK : 3 * TOK]
        send_far[:, at] = value[3 * TOK :]


def turn(places, grads):
    whole = pl.BlockSpec(memory_space=pltpu.VMEM)
    return pl.pallas_call(
        turn_kernel,
        out_shape=(
            jax.ShapeDtypeStruct((8 * SIDE, 4 * TOK), BF),
            jax.ShapeDtypeStruct((2 * TOK, 8 * SIDE), BF),
            jax.ShapeDtypeStruct((TOK, 8 * SIDE), BF),
            jax.ShapeDtypeStruct((TOK, 8 * SIDE), BF),
        ),
        in_specs=[TOKEN] + [whole] * 8,
        out_specs=(whole,) * 4,
        compiler_params=PARAMS,
        cost_estimate=cost(1000, 1000),
        name="turn",
    )(places, *grads)


def finish_kernel(gate_pre, up_pre, keep, far, *refs):
    gate_out, up_out = refs[-2:]
    hidden_grad = keep[...] + far[...].astype(F32)
    gate = gate_pre[...].astype(F32)
    up = up_pre[...].astype(F32)
    sig = 0.5 + 0.5 * jnp.tanh(0.5 * gate)
    swish = gate * sig
    gate_out[...] = (hidden_grad * up * (sig + swish * (1.0 - sig))).astype(BF)
    up_out[...] = (hidden_grad * swish).astype(BF)


def finish(gate_pre, up_pre, keep, far, start, keep_start, made):
    cols = far.shape[1]
    first, skip = start // TILE, keep_start // TILE
    wide = pl.BlockSpec((TOK, TILE), lambda n: (0, n + first))
    one = pl.BlockSpec((TOK, TILE), lambda n: (0, n))
    return pl.pallas_call(
        finish_kernel,
        out_shape=(jax.ShapeDtypeStruct(gate_pre.shape, BF),) * 2,
        grid=(cols // TILE,),
        in_specs=[wide, wide, pl.BlockSpec((TOK, TILE), lambda n: (0, n + skip)), one] + [ANY] * len(made),
        out_specs=(wide, wide),
        input_output_aliases={4 + i: i for i in range(len(made))},
        compiler_params=PARAMS,
        cost_estimate=cost(20 * TOK * cols, 16 * TOK * cols),
        name="finish",
    )(gate_pre, up_pre, keep, far, *made)


def per_device(out_grad, gate_pre, up_pre, down_tiles, down_scales):
    yh, c = lax.axis_index("yh"), lax.axis_index("c")
    yl, x = lax.axis_index("yl"), lax.axis_index("x")

    def block(r):
        other = 2 * (yh ^ (r >> 1)) + (c ^ (r & 1))
        return lax.dynamic_slice(out_grad, (0, other * SIDE), (TOK, SIDE))

    gate = gate_pre.astype(F32)
    h0 = (gate * jax.nn.sigmoid(gate) * up_pre.astype(F32)).astype(BF)
    hb, hc, hd = (h0[:, PARTS[k] : PARTS[k + 1]] for k in range(3))
    blocks = [block(r) for r in range(4)]
    down_tiles, *blocks = lax.optimization_barrier((down_tiles, *blocks))
    pieces = [
        blocks[0],
        lax.ppermute(blocks[2], "yh", SWAP),
        lax.ppermute(blocks[1], "c", SWAP),
        lax.ppermute(blocks[3], ("yh", "c"), [(i, 3 - i) for i in range(4)]),
    ]
    g = jnp.concatenate(pieces, axis=0)

    weight = dequantize(down_tiles, down_scales)
    weights = lax.all_gather(weight, "z", axis=0, tiled=True)

    gy = lax.ppermute(g, "yl", SWAP)
    g_m, g_p = shift(g, "x", 4, 1), shift(g, "x", 4, -1)
    hb1, hc1, hd1 = (lax.ppermute(h, "c", SWAP) for h in (hb, hc, hd))
    gy, g_m, g_p, hb, hb1 = lax.optimization_barrier((gy, g_m, g_p, hb, hb1))
    gy_m, gy_p = shift(gy, "x", 4, 1), shift(gy, "x", 4, -1)
    hb2 = lax.ppermute(hb, "yh", SWAP)
    hc, hb2, gy_m, gy_p, g_m, hc1 = lax.optimization_barrier((hc, hb2, gy_m, gy_p, g_m, hc1))
    hc2 = lax.ppermute(hc, "yh", SWAP)
    g_far, gy_far = shift(g_m, "x", 4, 1), shift(gy_p, "x", 4, -1)
    hb3 = lax.ppermute(hb2, "c", SWAP)
    g_far, gy_far, weights, hb3, hc2, hd, hd1 = lax.optimization_barrier(
        (g_far, gy_far, weights, hb3, hc2, hd, hd1)
    )
    hd2 = lax.ppermute(hd, "yh", SWAP)
    hc3 = lax.ppermute(hc2, "c", SWAP)
    partner_weights = lax.ppermute(weights, "c", SWAP)
    places = jnp.stack(
        [
            (yl ^ dy) * 4 + ((x + dx) & 3)
            for dy, dx in ((0, 0), (1, 0), (0, 3), (0, 1), (1, 3), (1, 1), (0, 2), (1, 2))
        ]
    ).astype(jnp.int32)
    turned, mine, *send = turn(places, (g, gy, g_m, g_p, gy_m, gy_p, g_far, gy_far))
    theirs = [lax.ppermute(v, "c", SWAP) for v in send]
    hd3 = lax.ppermute(hd2, "c", SWAP)
    partner_weights, turned, theirs, hc3, hd3 = lax.optimization_barrier(
        (partner_weights, turned, theirs, hc3, hd3)
    )
    hidden = (hb, hb2, hb1, hb3, hc, hc2, hc1, hc3, hd, hd2, hd1, hd3)
    down, places = down_partial(places, turned, hidden)
    total = lax.psum_scatter(down, "z", scatter_dimension=0, tiled=True).astype(F32)

    made, found = (), []
    for cuts in (CUTS[:2], CUTS[1:]):
        places, keep, *passed = hidden_partial(
            places, mine, theirs, weights, partner_weights, cuts
        )
        for start, value in zip(cuts, passed):
            far = lax.ppermute(value, "yh", SWAP)
            found.append((keep, far, start, start - cuts[0]))
    for keep, far, start, inside in found:
        made = finish(gate_pre, up_pre, keep, far, start, inside, made)
    return (*made, total)


def solution(mesh):
    fine = Mesh(mesh.devices.reshape(SIZES), AXES)
    spec = P(("z", "yh", "c"), ("yl", "x"))
    return jax.shard_map(
        per_device,
        mesh=fine,
        in_specs=(spec,) * 5,
        out_specs=(spec,) * 3,
        check_vma=False,
    )
```

time: 184 us -> 174 us (0.946)
  waiting for transfers between devices: 86.3 us -> 63.8 us
  starting transfers between devices: 23.6 us -> 29.8 us
  Pallas kernels: 47.1 us -> 51 us
    ppermute x11 -> x16, waiting for transfers between devices: 56.7 us -> 38.2 us  [the longest x3 16.6 us: per_device(): far = lax.ppermute(value, 'yh', SWAP)]
    ppermute x6, waiting for transfers between devices: 19.9 us -> 10.1 us  [shift(): lax.ppermute(value, axis, [(i, (i + by) % size) for i in range(size)])]
    ppermute x1, waiting for transfers between devices: 0.01 us -> 9.11 us  [per_device(): gy = lax.ppermute(g, 'yl', SWAP)]
    ppermute x11 -> x16, starting transfers between devices: 13.7 us -> 16.5 us  [the longest x3 3.85 us: per_device(): far = lax.ppermute(value, 'yh', SWAP)]
    ppermute x1, waiting for transfers between devices: 2.57 us -> 0.01 us  [per_device(): hb3 = lax.ppermute(hb2, 'c', SWAP)]
    ppermute x1, starting transfers between devices: 0.37 us -> 2.57 us  [per_device(): hb2 = lax.ppermute(hb, 'yh', SWAP)]
    pallas_call x4 -> x3, Pallas kernels: 23.1 us -> 24.9 us  [the longest x2 18.2 us: hidden_partial(): pl.pallas_call(functools.partial(up_kernel, spans), out_shape=(TOKEN_TYPE...]
    pallas_call x2 -> x3, Pallas kernels: 9.63 us -> 11 us  [finish(): pl.pallas_call(finish_kernel, out_shape=(jax.ShapeDtypeStruct(gate_pre.sh...]
  transfers between devices with their start and end apart: 22 -> 27, of which waited for: 12 -> 12; matrix products, arithmetic and copies ran while one was open for 2% -> 2% of each run, Pallas kernels for 26% -> 21%
where the time goes in v2:
time: 174 us; the launch traced here: 173 us
  waiting for transfers between devices  63.8 us (37%)
  Pallas kernels  51 us (29%)
  starting transfers between devices  29.8 us (17%)
  between operations  14.4 us (8%)
  local copies, waits for them, and re-layouts  7.26 us (4%)
  other arithmetic  6.37 us (4%)
    pallas_call x2, Pallas kernels, hidden_partial(): pl.pallas_call(functools.partial(up_kernel, spans), out_shape=(TOKEN_TYPE...  18.2 us
    ppermute x3, waiting for transfers between devices, per_device(): far = lax.ppermute(value, 'yh', SWAP)  16.6 us
    pallas_call x1, Pallas kernels, down_partial(): pl.pallas_call(down_kernel, out_shape=(jax.ShapeDtypeStruct((8 * SIDE, co...  15.1 us
    ppermute x1, waiting for transfers between devices, per_device(): hd2 = lax.ppermute(hd, 'yh', SWAP)  11.3 us
    pallas_call x3, Pallas kernels, finish(): pl.pallas_call(finish_kernel, out_shape=(jax.ShapeDtypeStruct(gate_pre.sh...  11 us
    ppermute x6, waiting for transfers between devices, shift(): lax.ppermute(value, axis, [(i, (i + by) % size) for i in range(size)])  10.1 us
    ppermute x1, waiting for transfers between devices, per_device(): gy = lax.ppermute(g, 'yl', SWAP)  9.11 us
    ppermute x6, starting transfers between devices, shift(): lax.ppermute(value, axis, [(i, (i + by) % size) for i in range(size)])  8.17 us
  transfers between devices with their start and end apart: 27, of which 12 were waited for; matrix products, arithmetic and copies ran while one was open for 2% of the time, Pallas kernels for 21%

profile of v2, /device:TPU:1, one launch (start us, length us, event | category | flops | bytes accessed | tf_op | source)
XLA Modules:
  0.0 172.7 jit_solution(420430038934836028)
XLA Ops:
  10.5 3.8 %collective-permute-start = (bf16[480,128]{1,0:T(8,128)(2,1)S(1)}, bf16[480,128]{1,0:T(8,128)(2,1)S(1)}, u32[]{:S(2)}, u32[]{:S(2)}) collective-permute-start(bf16[480,128]{1,0:T(8,128)(2,1)S(1)} %get-tuple-element.51), channel_id=1, source_target_pairs={{0,16},{16,0},{1,17},{17,1},{2,18},{18,2},{3,19},{19,3},{4,20},{20... | collective-permute-start | bytes 368648 | tf_op jit(solution)/shard_map/ppermute | solution.py:241
  17.0 2.5 %fusion.4 = bf16[480,1792]{1,0:T(8,128)(2,1)S(1)} fusion(bf16[480,1792]{1,0:T(8,128)(2,1)} %up_pre.5, bf16[480,1792]{1,0:T(8,128)(2,1)S(1)} %copy-done.1), kind=kLoop, calls=%fused_computation.6 | loop fusion | flops 6881280 | bytes 5160960 | tf_op jit(solution)/shard_map/convert_element_type | solution.py:235
  20.3 1.9 %collective-permute-done.2 = bf16[480,128]{1,0:T(8,128)(2,1)S(1)} collective-permute-done((bf16[480,128]{1,0:T(8,128)(2,1)S(1)}, bf16[480,128]{1,0:T(8,128)(2,1)S(1)}, u32[]{:S(2)}, u32[]{:S(2)}) %collective-permute-start.2) | collective-permute-done | bytes 122912 | tf_op jit(solution)/shard_map/ppermute | solution.py:243
  25.9 9.1 %collective-permute-done.3.refs_1_ = bf16[1920,128]{1,0:T(8,128)(2,1)S(1)} collective-permute-done((bf16[1920,128]{1,0:T(8,128)(2,1)S(1)}, bf16[1920,128]{1,0:T(8,128)(2,1)S(1)}, u32[]{:S(2)}, u32[]{:S(2)}) %collective-permute-start.3) | collective-permute-done | bytes 491552 | tf_op jit(solution)/shard_map/ppermute | solution.py:250
  36.3 2.6 %collective-permute-start.7 = (bf16[480,512]{1,0:T(8,128)(2,1)S(1)}, bf16[480,512]{1,0:T(8,128)(2,1)S(1)}, u32[]{:S(2)}, u32[]{:S(2)}) collective-permute-start(bf16[480,512]{1,0:T(8,128)(2,1)S(1)} %get-tuple-element.54.refs_1_), channel_id=1, source_target_pairs={{0,16},{16,0},{1,17},{17,1},{2,18},{18,2},{3,19},{19,3},{4,20},{20... | collective-permute-start | bytes 1474568 | tf_op jit(solution)/shard_map/ppermute | solution.py:255
  43.3 6.4 %collective-permute-done.7.refs_2_ = bf16[480,512]{1,0:T(8,128)(2,1)S(1)} collective-permute-done((bf16[480,512]{1,0:T(8,128)(2,1)S(1)}, bf16[480,512]{1,0:T(8,128)(2,1)S(1)}, u32[]{:S(2)}, u32[]{:S(2)}) %collective-permute-start.7) | collective-permute-done | bytes 491552 | tf_op jit(solution)/shard_map/ppermute | solution.py:255
  49.7 2.2 %collective-permute-done.8.refs_4_ = bf16[1920,128]{1,0:T(8,128)(2,1)S(1)} collective-permute-done((bf16[1920,128]{1,0:T(8,128)(2,1)S(1)}, bf16[1920,128]{1,0:T(8,128)(2,1)S(1)}, u32[]{:S(2)}, u32[]{:S(2)}) %collective-permute-start.8) | collective-permute-done | bytes 491552 | tf_op jit(solution)/shard_map/ppermute | solution.py:38
  52.0 2.7 %collective-permute-start.12 = (bf16[1920,128]{1,0:T(8,128)(2,1)S(1)}, bf16[1920,128]{1,0:T(8,128)(2,1)S(1)}, u32[]{:S(2)}, u32[]{:S(2)}) collective-permute-start(bf16[1920,128]{1,0:T(8,128)(2,1)S(1)} %collective-permute-done.9.refs_5_), channel_id=1, source_target_pairs={{0,3},{1,0},{2,1},{3,2},{4,7},{5,4},{6,5},{7,6},{8,11},{9,8},{10,9... | collective-permute-start | bytes 1474568 | tf_op jit(solution)/shard_map/ppermute | solution.py:38
  54.6 2.4 %collective-permute-start.13 = (bf16[480,512]{1,0:T(8,128)(2,1)S(1)}, bf16[480,512]{1,0:T(8,128)(2,1)S(1)}, u32[]{:S(2)}, u32[]{:S(2)}) collective-permute-start(bf16[480,512]{1,0:T(8,128)(2,1)S(1)} %collective-permute-done.7.refs_2_), channel_id=1, source_target_pairs={{0,8},{8,0},{1,9},{9,1},{2,10},{10,2},{3,11},{11,3},{4,12},{12,4},... | collective-permute-start | bytes 1474568 | tf_op jit(solution)/shard_map/ppermute | solution.py:259
  57.5 6.6 %collective-permute-done.11.refs_6_ = bf16[1920,128]{1,0:T(8,128)(2,1)S(1)} collective-permute-done((bf16[1920,128]{1,0:T(8,128)(2,1)S(1)}, bf16[1920,128]{1,0:T(8,128)(2,1)S(1)}, u32[]{:S(2)}, u32[]{:S(2)}) %collective-permute-start.11) | collective-permute-done | bytes 491552 | tf_op jit(solution)/shard_map/ppermute | solution.py:38
  65.9 5.6 %collective-permute-done.14.refs_6_ = bf16[480,512]{1,0:T(8,128)(2,1)} collective-permute-done((bf16[480,512]{1,0:T(8,128)(2,1)S(1)}, bf16[480,512]{1,0:T(8,128)(2,1)}, u32[]{:S(2)}, u32[]{:S(2)}) %collective-permute-start.14) | collective-permute-done | bytes 491552 | tf_op jit(solution)/shard_map/ppermute | solution.py:257
  73.3 6.7 %turn.1 = (bf16[1024,1920]{1,0:T(8,128)(2,1)}, bf16[960,1024]{1,0:T(8,128)(2,1)}, bf16[480,1024]{1,0:T(8,128)(2,1)}, bf16[480,1024]{1,0:T(8,128)(2,1)}) custom-call(s32[8]{0:T(128)} %stack.35.places, bf16[1920,128]{1,0:T(8,128)(2,1)} %copy-done.7, bf16[1920,128]{1,0:T(8,128)(2,1)} %copy-done.15, bf16[1920,128]{1,0:T(8,128)(2,1)} %copy-done.16, ...), custom_call_target="tpu_custom_call" | custom-call | flops 1000 | bytes 1000 | tf_op jit(solution)/shard_map/turn/pallas_call | solution.py:181
  80.7 11.3 %collective-permute-done.20.refs_10_ = bf16[480,768]{1,0:T(8,128)(2,1)} collective-permute-done((bf16[480,768]{1,0:T(8,128)(2,1)S(1)}, bf16[480,768]{1,0:T(8,128)(2,1)}, u32[]{:S(2)}, u32[]{:S(2)}) %collective-permute-start.20) | collective-permute-done | bytes 737312 | tf_op jit(solution)/shard_map/ppermute | solution.py:263
  92.8 2.8 %collective-permute-done.19.refs_8_ = bf16[480,512]{1,0:T(8,128)(2,1)S(1)} collective-permute-done((bf16[480,512]{1,0:T(8,128)(2,1)}, bf16[480,512]{1,0:T(8,128)(2,1)S(1)}, u32[]{:S(2)}, u32[]{:S(2)}) %collective-permute-start.19) | collective-permute-done | bytes 491552 | tf_op jit(solution)/shard_map/ppermute | solution.py:264
  96.6 15.1 %down_partial.1 = (bf16[1024,1792]{1,0:T(8,128)(2,1)}, s32[8]{0:T(128)}) custom-call(s32[8]{0:T(128)} %stack.35.places, bf16[1024,1920]{1,0:T(8,128)(2,1)} %get-tuple-element.72.refs_0_, bf16[480,512]{1,0:T(8,128)(2,1)} %copy-done.5, bf16[480,512]{1,0:T(8,128)(2,1)} %copy-done.14, bf16[480,512]{1,0:T(8,128)(2,1)} %copy-done.12, bf16[480,512]{1,0:T(8,128)(2,1)} %copy-done.18, ...), custom_call_target="tpu_custom_call" | custom-call | flops 1000 | bytes 1000 | tf_op jit(solution)/shard_map/down_partial/pallas_call | solution.py:84
  111.8 8.2 %hidden_partial.2 = (s32[8]{0:T(128)}, f32[480,768]{1,0:T(8,128)}, bf16[480,768]{1,0:T(8,128)(2,1)}) custom-call(s32[8]{0:T(128)} %get-tuple-element.79.places, bf16[960,1024]{1,0:T(8,128)(2,1)} %get-tuple-element.80.mine, bf16[480,1024]{1,0:T(8,128)(2,1)} %copy-done.2, bf16[480,1024]{1,0:T(8,128)(2,1)} %copy-done.3, ...), custom_call_target="tpu_custom_call" | custom-call | flops 1000 | bytes 1000 | tf_op jit(solution)/shard_map/hidden_partial/pallas_call | solution.py:147
  120.8 10.0 %hidden_partial.3 = (s32[8]{0:T(128)}, f32[480,1024]{1,0:T(8,128)}, bf16[480,768]{1,0:T(8,128)(2,1)}, bf16[480,256]{1,0:T(8,128)(2,1)}) custom-call(s32[8]{0:T(128)} %get-tuple-element.84.places, bf16[960,1024]{1,0:T(8,128)(2,1)} %get-tuple-element.80.mine, bf16[480,1024]{1,0:T(8,128)(2,1)} %copy-done.2, bf16[480,1024]{1,0:T(8,128)(2,1)} %copy-done.3, ...), custom_call_target="tpu_custom_call" | custom-call | flops 1000 | bytes 1000 | tf_op jit(solution)/shard_map/hidden_partial/pallas_call | solution.py:147
  130.7 2.7 %collective-permute-start.23 = (bf16[480,768]{1,0:T(8,128)(2,1)}, bf16[480,768]{1,0:T(8,128)(2,1)S(1)}, u32[]{:S(2)}, u32[]{:S(2)}) collective-permute-start(bf16[480,768]{1,0:T(8,128)(2,1)} %get-tuple-element.87), channel_id=1, source_target_pairs={{0,16},{16,0},{1,17},{17,1},{2,18},{18,2},{3,19},{19,3},{4,20},{20... | collective-permute-start | bytes 2211848 | tf_op jit(solution)/shard_map/ppermute | solution.py:288
  133.8 5.9 %collective-permute-done.24.far = bf16[480,768]{1,0:T(8,128)(2,1)S(1)} collective-permute-done((bf16[480,768]{1,0:T(8,128)(2,1)}, bf16[480,768]{1,0:T(8,128)(2,1)S(1)}, u32[]{:S(2)}, u32[]{:S(2)}) %collective-permute-start.24) | collective-permute-done | bytes 737312 | tf_op jit(solution)/shard_map/ppermute | solution.py:288
  140.6 4.3 %finish.3 = (bf16[480,1792]{1,0:T(8,128)(2,1)}, bf16[480,1792]{1,0:T(8,128)(2,1)}) custom-call(bf16[480,1792]{1,0:T(8,128)(2,1)} %gate_pre.5, bf16[480,1792]{1,0:T(8,128)(2,1)} %up_pre.5, f32[480,768]{1,0:T(8,128)} %get-tuple-element.88.keep, bf16[480,768]{1,0:T(8,128)(2,1)} %copy-done.8), custom_call_target="tpu_custom_call" | custom-call | flops 7372800 | bytes 5898240 | tf_op jit(solution)/shard_map/finish/pallas_call | solution.py:213
  144.9 10.6 %collective-permute-done.23.far = bf16[480,768]{1,0:T(8,128)(2,1)S(1)} collective-permute-done((bf16[480,768]{1,0:T(8,128)(2,1)}, bf16[480,768]{1,0:T(8,128)(2,1)S(1)}, u32[]{:S(2)}, u32[]{:S(2)}) %collective-permute-start.23) | collective-permute-done | bytes 737312 | tf_op jit(solution)/shard_map/ppermute | solution.py:288
  156.4 4.3 %finish.4 = (bf16[480,1792]{1,0:T(8,128)(2,1)}, bf16[480,1792]{1,0:T(8,128)(2,1)}) custom-call(bf16[480,1792]{1,0:T(8,128)(2,1)} %gate_pre.5, bf16[480,1792]{1,0:T(8,128)(2,1)} %up_pre.5, f32[480,1024]{1,0:T(8,128)} %get-tuple-element.85.keep, bf16[480,768]{1,0:T(8,128)(2,1)} %copy-done.9, ...), custom_call_target="tpu_custom_call", output_to_operand_aliasing={{0}: (4, {}), {1}: (5, {})} | custom-call | flops 7372800 | bytes 5898240 | tf_op jit(solution)/shard_map/finish/pallas_call | solution.py:213
  161.4 2.4 %finish.5 = (bf16[480,1792]{1,0:T(8,128)(2,1)}, bf16[480,1792]{1,0:T(8,128)(2,1)}) custom-call(bf16[480,1792]{1,0:T(8,128)(2,1)} %gate_pre.5, bf16[480,1792]{1,0:T(8,128)(2,1)} %up_pre.5, f32[480,1024]{1,0:T(8,128)} %get-tuple-element.85.keep, bf16[480,256]{1,0:T(8,128)(2,1)} %copy-done.24, ...), custom_call_target="tpu_custom_call", output_to_operand_aliasing={{0}: (4, {}), {1}: (5, {})} | custom-call | flops 2457600 | bytes 1966080 | tf_op jit(solution)/shard_map/finish/pallas_call | solution.py:213
  163.8 2.0 %convert_element_type.23 = f32[128,1792]{1,0:T(8,128)} convert(bf16[128,1792]{1,0:T(8,128)(2,1)} %reduce-scatter.2.cloned.1.call-done) | non-fusion elementwise | flops 229376 | bytes 1376256 | tf_op jit(solution)/shard_map/convert_element_type | solution.py:280
  (101 shorter events, 26.3 us)
Async XLA Ops:
  7.2 64.3 %all-gather.2.cloned.1.call-start = ((), (), s32[]{:S(2)}) async-start(), calls=%async_computation.1 | async-start | bytes 4128768 | tf_op jit(solution)/shard_map/all_gather | solution.py:248
  10.5 153.3 %reduce-scatter.2.cloned.1.call-start = ((), (), s32[]{:S(2)}) async-start(), calls=%async_computation.2 | async-start | bytes 4128768 | tf_op jit(solution)/shard_map/reduce_scatter | solution.py:280
  10.5 9.7 %collective-permute-start = (bf16[480,128]{1,0:T(8,128)(2,1)S(1)}, bf16[480,128]{1,0:T(8,128)(2,1)S(1)}, u32[]{:S(2)}, u32[]{:S(2)}) collective-permute-start(bf16[480,128]{1,0:T(8,128)(2,1)S(1)} %get-tuple-element.51), channel_id=1, source_target_pairs={{0,16},{16,0},{1,17},{17,1},{2,18},{18,2},{3,19},{19,3},{4,20},{20... | collective-permute-start | bytes 368648 | tf_op jit(solution)/shard_map/ppermute | solution.py:241
  15.3 6.9 %collective-permute-start.2 = (bf16[480,128]{1,0:T(8,128)(2,1)S(1)}, bf16[480,128]{1,0:T(8,128)(2,1)S(1)}, u32[]{:S(2)}, u32[]{:S(2)}) collective-permute-start(bf16[480,128]{1,0:T(8,128)(2,1)S(1)} %get-tuple-element.53), channel_id=1, source_target_pairs={{0,24},{8,16},{16,8},{24,0},{1,25},{9,17},{17,9},{25,1},{2,26},{10... | collective-permute-start | bytes 368648 | tf_op jit(solution)/shard_map/ppermute | solution.py:243
  19.6 6.3 %collective-permute-start.6 = (bf16[480,512]{1,0:T(8,128)(2,1)S(1)}, bf16[480,512]{1,0:T(8,128)(2,1)S(1)}, u32[]{:S(2)}, u32[]{:S(2)}) collective-permute-start(bf16[480,512]{1,0:T(8,128)(2,1)S(1)} %get-tuple-element.54.refs_1_), channel_id=1, source_target_pairs={{0,8},{8,0},{1,9},{9,1},{2,10},{10,2},{3,11},{11,3},{4,12},{12,4},... | collective-permute-start | bytes 1474568 | tf_op jit(solution)/shard_map/ppermute | solution.py:252
  22.2 12.8 %collective-permute-start.3 = (bf16[1920,128]{1,0:T(8,128)(2,1)S(1)}, bf16[1920,128]{1,0:T(8,128)(2,1)S(1)}, u32[]{:S(2)}, u32[]{:S(2)}) collective-permute-start(bf16[1920,128]{1,0:T(8,128)(2,1)S(1)} %constant_dynamic-update-slice_fusion.refs_0_), channel_id=1, source_target_pairs={{0,4},{4,0},{1,5},{5,1},{2,6},{6,2},{3,7},{7,3},{8,12},{12,8},{9,1... | collective-permute-start | bytes 1474568 | tf_op jit(solution)/shard_map/ppermute | solution.py:250
  22.3 14.0 %collective-permute-start.4 = (bf16[1920,128]{1,0:T(8,128)(2,1)S(1)}, bf16[1920,128]{1,0:T(8,128)(2,1)S(1)}, u32[]{:S(2)}, u32[]{:S(2)}) collective-permute-start(bf16[1920,128]{1,0:T(8,128)(2,1)S(1)} %constant_dynamic-update-slice_fusion.refs_0_), channel_id=1, source_target_pairs={{0,1},{1,2},{2,3},{3,0},{4,5},{5,6},{6,7},{7,4},{8,9},{9,10},{10,1... | collective-permute-start | bytes 1474568 | tf_op jit(solution)/shard_map/ppermute | solution.py:38
  23.5 12.8 %collective-permute-start.5 = (bf16[1920,128]{1,0:T(8,128)(2,1)S(1)}, bf16[1920,128]{1,0:T(8,128)(2,1)S(1)}, u32[]{:S(2)}, u32[]{:S(2)}) collective-permute-start(bf16[1920,128]{1,0:T(8,128)(2,1)S(1)} %constant_dynamic-update-slice_fusion.refs_0_), channel_id=1, source_target_pairs={{0,3},{1,0},{2,1},{3,2},{4,7},{5,4},{6,5},{7,6},{8,11},{9,8},{10,9... | collective-permute-start | bytes 1474568 | tf_op jit(solution)/shard_map/ppermute | solution.py:38
  25.1 18.2 %collective-permute-start.10 = (bf16[480,512]{1,0:T(8,128)(2,1)S(1)}, bf16[480,512]{1,0:T(8,128)(2,1)S(1)}, u32[]{:S(2)}, u32[]{:S(2)}) collective-permute-start(bf16[480,512]{1,0:T(8,128)(2,1)S(1)} %get-tuple-element.61.refs_5_), channel_id=1, source_target_pairs={{0,8},{8,0},{1,9},{9,1},{2,10},{10,2},{3,11},{11,3},{4,12},{12,4},... | collective-permute-start | bytes 1474568 | tf_op jit(solution)/shard_map/ppermute | solution.py:252
  36.3 13.4 %collective-permute-start.7 = (bf16[480,512]{1,0:T(8,128)(2,1)S(1)}, bf16[480,512]{1,0:T(8,128)(2,1)S(1)}, u32[]{:S(2)}, u32[]{:S(2)}) collective-permute-start(bf16[480,512]{1,0:T(8,128)(2,1)S(1)} %get-tuple-element.54.refs_1_), channel_id=1, source_target_pairs={{0,16},{16,0},{1,17},{17,1},{2,18},{18,2},{3,19},{19,3},{4,20},{20... | collective-permute-start | bytes 1474568 | tf_op jit(solution)/shard_map/ppermute | solution.py:255
  38.9 13.0 %collective-permute-start.8 = (bf16[1920,128]{1,0:T(8,128)(2,1)S(1)}, bf16[1920,128]{1,0:T(8,128)(2,1)S(1)}, u32[]{:S(2)}, u32[]{:S(2)}) collective-permute-start(bf16[1920,128]{1,0:T(8,128)(2,1)S(1)} %collective-permute-done.3.refs_1_), channel_id=1, source_target_pairs={{0,1},{1,2},{2,3},{3,0},{4,5},{5,6},{6,7},{7,4},{8,9},{9,10},{10,1... | collective-permute-start | bytes 1474568 | tf_op jit(solution)/shard_map/ppermute | solution.py:38
  39.7 12.2 %collective-permute-start.9 = (bf16[1920,128]{1,0:T(8,128)(2,1)S(1)}, bf16[1920,128]{1,0:T(8,128)(2,1)S(1)}, u32[]{:S(2)}, u32[]{:S(2)}) collective-permute-start(bf16[1920,128]{1,0:T(8,128)(2,1)S(1)} %collective-permute-done.3.refs_1_), channel_id=1, source_target_pairs={{0,3},{1,0},{2,1},{3,2},{4,7},{5,4},{6,5},{7,6},{8,11},{9,8},{10,9... | collective-permute-start | bytes 1474568 | tf_op jit(solution)/shard_map/ppermute | solution.py:38
  41.6 15.9 %collective-permute-start.15 = (bf16[480,768]{1,0:T(8,128)(2,1)S(1)}, bf16[480,768]{1,0:T(8,128)(2,1)S(1)}, u32[]{:S(2)}, u32[]{:S(2)}) collective-permute-start(bf16[480,768]{1,0:T(8,128)(2,1)S(1)} %slice.14.refs_9_), channel_id=1, source_target_pairs={{0,8},{8,0},{1,9},{9,1},{2,10},{10,2},{3,11},{11,3},{4,12},{12,4},... | collective-permute-start | bytes 2211848 | tf_op jit(solution)/shard_map/ppermute | solution.py:252
  51.9 12.3 %collective-permute-start.11 = (bf16[1920,128]{1,0:T(8,128)(2,1)S(1)}, bf16[1920,128]{1,0:T(8,128)(2,1)S(1)}, u32[]{:S(2)}, u32[]{:S(2)}) collective-permute-start(bf16[1920,128]{1,0:T(8,128)(2,1)S(1)} %collective-permute-done.4.refs_2_), channel_id=1, source_target_pairs={{0,1},{1,2},{2,3},{3,0},{4,5},{5,6},{6,7},{7,4},{8,9},{9,10},{10,1... | collective-permute-start | bytes 1474568 | tf_op jit(solution)/shard_map/ppermute | solution.py:38
  52.0 12.2 %collective-permute-start.12 = (bf16[1920,128]{1,0:T(8,128)(2,1)S(1)}, bf16[1920,128]{1,0:T(8,128)(2,1)S(1)}, u32[]{:S(2)}, u32[]{:S(2)}) collective-permute-start(bf16[1920,128]{1,0:T(8,128)(2,1)S(1)} %collective-permute-done.9.refs_5_), channel_id=1, source_target_pairs={{0,3},{1,0},{2,1},{3,2},{4,7},{5,4},{6,5},{7,6},{8,11},{9,8},{10,9... | collective-permute-start | bytes 1474568 | tf_op jit(solution)/shard_map/ppermute | solution.py:38
  54.6 9.5 %collective-permute-start.13 = (bf16[480,512]{1,0:T(8,128)(2,1)S(1)}, bf16[480,512]{1,0:T(8,128)(2,1)S(1)}, u32[]{:S(2)}, u32[]{:S(2)}) collective-permute-start(bf16[480,512]{1,0:T(8,128)(2,1)S(1)} %collective-permute-done.7.refs_2_), channel_id=1, source_target_pairs={{0,8},{8,0},{1,9},{9,1},{2,10},{10,2},{3,11},{11,3},{4,12},{12,4},... | collective-permute-start | bytes 1474568 | tf_op jit(solution)/shard_map/ppermute | solution.py:259
  57.0 14.5 %collective-permute-start.14 = (bf16[480,512]{1,0:T(8,128)(2,1)S(1)}, bf16[480,512]{1,0:T(8,128)(2,1)}, u32[]{:S(2)}, u32[]{:S(2)}) collective-permute-start(bf16[480,512]{1,0:T(8,128)(2,1)S(1)} %get-tuple-element.61.refs_5_), channel_id=1, source_target_pairs={{0,16},{16,0},{1,17},{17,1},{2,18},{18,2},{3,19},{19,3},{4,20},{20... | collective-permute-start | bytes 1474568 | tf_op jit(solution)/shard_map/ppermute | solution.py:257
  71.5 24.1 %collective-permute-start.16 = (bf16[1024,1792]{1,0:T(8,128)(2,1)}, bf16[1024,1792]{1,0:T(8,128)(2,1)}, u32[]{:S(2)}, u32[]{:S(2)}) collective-permute-start(bf16[1024,1792]{1,0:T(8,128)(2,1)} %all-gather.2.cloned.1.call-done.weights), channel_id=1, source_target_pairs={{0,8},{8,0},{1,9},{9,1},{2,10},{10,2},{3,11},{11,3},{4,12},{12,4},... | collective-permute-start | bytes 11010056 | tf_op jit(solution)/shard_map/ppermute | solution.py:265
  72.3 19.7 %collective-permute-start.20 = (bf16[480,768]{1,0:T(8,128)(2,1)S(1)}, bf16[480,768]{1,0:T(8,128)(2,1)}, u32[]{:S(2)}, u32[]{:S(2)}) collective-permute-start(bf16[480,768]{1,0:T(8,128)(2,1)S(1)} %slice.14.refs_9_), channel_id=1, source_target_pairs={{0,16},{16,0},{1,17},{17,1},{2,18},{18,2},{3,19},{19,3},{4,20},{20... | collective-permute-start | bytes 2211848 | tf_op jit(solution)/shard_map/ppermute | solution.py:263
  80.1 15.5 %collective-permute-start.17 = (bf16[480,1024]{1,0:T(8,128)(2,1)}, bf16[480,1024]{1,0:T(8,128)(2,1)S(1)}, u32[]{:S(2)}, u32[]{:S(2)}) collective-permute-start(bf16[480,1024]{1,0:T(8,128)(2,1)} %get-tuple-element.68), channel_id=1, source_target_pairs={{0,8},{8,0},{1,9},{9,1},{2,10},{10,2},{3,11},{11,3},{4,12},{12,4},... | collective-permute-start | bytes 2949128 | tf_op jit(solution)/shard_map/ppermute | solution.py:273
  80.5 15.1 %collective-permute-start.18 = (bf16[480,1024]{1,0:T(8,128)(2,1)}, bf16[480,1024]{1,0:T(8,128)(2,1)S(1)}, u32[]{:S(2)}, u32[]{:S(2)}) collective-permute-start(bf16[480,1024]{1,0:T(8,128)(2,1)} %get-tuple-element.69), channel_id=1, source_target_pairs={{0,8},{8,0},{1,9},{9,1},{2,10},{10,2},{3,11},{11,3},{4,12},{12,4},... | collective-permute-start | bytes 2949128 | tf_op jit(solution)/shard_map/ppermute | solution.py:273
  120.0 19.7 %collective-permute-start.24 = (bf16[480,768]{1,0:T(8,128)(2,1)}, bf16[480,768]{1,0:T(8,128)(2,1)S(1)}, u32[]{:S(2)}, u32[]{:S(2)}) collective-permute-start(bf16[480,768]{1,0:T(8,128)(2,1)} %get-tuple-element.89), channel_id=1, source_target_pairs={{0,16},{16,0},{1,17},{17,1},{2,18},{18,2},{3,19},{19,3},{4,20},{20... | collective-permute-start | bytes 2211848 | tf_op jit(solution)/shard_map/ppermute | solution.py:288
  130.7 24.8 %collective-permute-start.23 = (bf16[480,768]{1,0:T(8,128)(2,1)}, bf16[480,768]{1,0:T(8,128)(2,1)S(1)}, u32[]{:S(2)}, u32[]{:S(2)}) collective-permute-start(bf16[480,768]{1,0:T(8,128)(2,1)} %get-tuple-element.87), channel_id=1, source_target_pairs={{0,16},{16,0},{1,17},{17,1},{2,18},{18,2},{3,19},{19,3},{4,20},{20... | collective-permute-start | bytes 2211848 | tf_op jit(solution)/shard_map/ppermute | solution.py:288
  133.4 27.3 %collective-permute-start.22 = (bf16[480,256]{1,0:T(8,128)(2,1)}, bf16[480,256]{1,0:T(8,128)(2,1)S(1)}, u32[]{:S(2)}, u32[]{:S(2)}) collective-permute-start(bf16[480,256]{1,0:T(8,128)(2,1)} %get-tuple-element.86), channel_id=1, source_target_pairs={{0,16},{16,0},{1,17},{17,1},{2,18},{18,2},{3,19},{19,3},{4,20},{20... | collective-permute-start | bytes 737288 | tf_op jit(solution)/shard_map/ppermute | solution.py:288
  (28 other events, 425.4 us)
Sparse Core Ops, SparseCore 0:
  10.6 53.6 all-gather.1
  111.9 49.5 reduce-scatter.1

commit v3 on v2

--- a/solution.py
+++ b/solution.py
@@ -15,7 +15,7 @@
 SIDE = 128
 TILE = 256
 PARTS = (0, 512, 1024, 1792)
-CUTS = (0, 768, 1536, 1792)
+CUTS = (0, 512, 1024, 1536, 1792)
 SWAP = [(0, 1), (1, 0)]
 PARAMS = pltpu.CompilerParams(vmem_limit_bytes=60 * 1024 * 1024)
 ANY = pl.BlockSpec(memory_space=pl.ANY)
@@ -194,8 +194,10 @@
     )(places, *grads)
 
 
-def finish_kernel(gate_pre, up_pre, keep, far, *refs):
-    gate_out, up_out = refs[-2:]
+def finish_kernel(last, gate_pre, up_pre, keep, far, *refs):
+    gate_out, up_out = refs[-3:-1] if last else refs[-2:]
+    if last:
+        refs[-1][...] = refs[0][...].astype(F32)
     hidden_grad = keep[...] + far[...].astype(F32)
     gate = gate_pre[...].astype(F32)
     up = up_pre[...].astype(F32)
@@ -205,22 +207,27 @@
     up_out[...] = (hidden_grad * swish).astype(BF)
 
 
-def finish(gate_pre, up_pre, keep, far, start, keep_start, made):
+def finish(gate_pre, up_pre, keep, far, start, keep_start, made, last=()):
     cols = far.shape[1]
     first, skip = start // TILE, keep_start // TILE
     wide = pl.BlockSpec((TOK, TILE), lambda n: (0, n + first))
     one = pl.BlockSpec((TOK, TILE), lambda n: (0, n))
+    kept = pl.BlockSpec((TOK, TILE), lambda n: (0, n + skip))
+    whole = [pl.BlockSpec(v.shape, lambda n: (0, 0)) for v in last]
     return pl.pallas_call(
-        finish_kernel,
-        out_shape=(jax.ShapeDtypeStruct(gate_pre.shape, BF),) * 2,
+        functools.partial(finish_kernel, len(last)),
+        out_shape=(
+            *(jax.ShapeDtypeStruct(gate_pre.shape, BF),) * 2,
+            *(jax.ShapeDtypeStruct(v.shape, F32) for v in last),
+        ),
         grid=(cols // TILE,),
-        in_specs=[wide, wide, pl.BlockSpec((TOK, TILE), lambda n: (0, n + skip)), one] + [ANY] * len(made),
-        out_specs=(wide, wide),
-        input_output_aliases={4 + i: i for i in range(len(made))},
+        in_specs=[wide, wide, kept, one] + whole + [ANY] * len(made),
+        out_specs=(wide, wide, *whole),
+        input_output_aliases={4 + len(last) + i: i for i in range(len(made))},
         compiler_params=PARAMS,
         cost_estimate=cost(20 * TOK * cols, 16 * TOK * cols),
         name="finish",
-    )(gate_pre, up_pre, keep, far, *made)
+    )(gate_pre, up_pre, keep, far, *last, *made)
 
 
 def per_device(out_grad, gate_pre, up_pre, down_tiles, down_scales):
@@ -253,7 +260,8 @@
     gy, g_m, g_p, hb, hb1 = lax.optimization_barrier((gy, g_m, g_p, hb, hb1))
     gy_m, gy_p = shift(gy, "x", 4, 1), shift(gy, "x", 4, -1)
     hb2 = lax.ppermute(hb, "yh", SWAP)
-    hc, hb2, gy_m, gy_p, g_m, hc1 = lax.optimization_barrier((hc, hb2, gy_m, gy_p, g_m, hc1))
+    hc, hb2, hc1 = lax.optimization_barrier((hc, hb2, hc1))
+    g_m, gy_m = lax.optimization_barrier((g_m, gy_m))
     hc2 = lax.ppermute(hc, "yh", SWAP)
     g_far, gy_far = shift(g_m, "x", 4, 1), shift(gy_p, "x", 4, -1)
     hb3 = lax.ppermute(hb2, "c", SWAP)
@@ -277,7 +285,7 @@
     )
     hidden = (hb, hb2, hb1, hb3, hc, hc2, hc1, hc3, hd, hd2, hd1, hd3)
     down, places = down_partial(places, turned, hidden)
-    total = lax.psum_scatter(down, "z", scatter_dimension=0, tiled=True).astype(F32)
+    total = lax.psum_scatter(down, "z", scatter_dimension=0, tiled=True)
 
     made, found = (), []
     for cuts in (CUTS[:2], CUTS[1:]):
@@ -288,8 +296,9 @@
             far = lax.ppermute(value, "yh", SWAP)
             found.append((keep, far, start, start - cuts[0]))
     for keep, far, start, inside in found:
-        made = finish(gate_pre, up_pre, keep, far, start, inside, made)
-    return (*made, total)
+        last = (total,) if start == CUTS[-2] else ()
+        made = finish(gate_pre, up_pre, keep, far, start, inside, made, last)
+    return made
 
 
 def solution(mesh):

time: 174 us -> 170 us (0.977)
  waiting for transfers between devices: 63.8 us -> 58.8 us
  starting transfers between devices: 29.8 us -> 34.7 us
  other arithmetic: 6.37 us -> 4.37 us
    ppermute x6, waiting for transfers between devices: 10.1 us -> 3.19 us  [shift(): lax.ppermute(value, axis, [(i, (i + by) % size) for i in range(size)])]
    ppermute x1, waiting for transfers between devices: 5.58 us -> 9.16 us  [per_device(): hc2 = lax.ppermute(hc, 'yh', SWAP)]
    ppermute x3 -> x4, waiting for transfers between devices: 16.6 us -> 13.9 us  [per_device(): far = lax.ppermute(value, 'yh', SWAP)]
    ppermute x3 -> x4, starting transfers between devices: 3.85 us -> 6.38 us  [per_device(): far = lax.ppermute(value, 'yh', SWAP)]
    ppermute x1, starting transfers between devices: 0.48 us -> 2.49 us  [per_device(): hc2 = lax.ppermute(hc, 'yh', SWAP)]
    convert_element_type x1 -> x0, other arithmetic: 2 us -> none  [per_device(): lax.psum_scatter(down, 'z', scatter_dimension=0, tiled=True).astype(F32)]
    reduce_scatter x1, waiting for transfers between devices: 0.01 us -> 1.91 us  [per_device(): total = lax.psum_scatter(down, 'z', scatter_dimension=0, tiled=True)]
    unnamed x53 -> x57, local copies, waits for them, and re-layouts: 5.24 us -> 4.41 us
  transfers between devices with their start and end apart: 27 -> 28, of which waited for: 12 -> 13; matrix products, arithmetic and copies ran while one was open for 2% -> 2% of each run, Pallas kernels for 21% -> 19%
where the time goes in v3:
time: 170 us
  waiting for transfers between devices  58.8 us (35%)
  Pallas kernels  51 us (30%)
  starting transfers between devices  34.7 us (20%)
  between operations  14.4 us (8%)
  local copies, waits for them, and re-layouts  6.54 us (4%)
  other arithmetic  4.37 us (3%)
    pallas_call x2, Pallas kernels, hidden_partial(): pl.pallas_call(functools.partial(up_kernel, spans), out_shape=(TOKEN_TYPE...  18 us
    pallas_call x1, Pallas kernels, down_partial(): pl.pallas_call(down_kernel, out_shape=(jax.ShapeDtypeStruct((8 * SIDE, co...  15.1 us
    ppermute x4, waiting for transfers between devices, per_device(): far = lax.ppermute(value, 'yh', SWAP)  13.9 us
    pallas_call x4, Pallas kernels, finish(): pl.pallas_call(functools.partial(finish_kernel, len(last)), out_shape=(*(...  11.2 us
    ppermute x1, waiting for transfers between devices, per_device(): hd2 = lax.ppermute(hd, 'yh', SWAP)  10.5 us
    ppermute x1, waiting for transfers between devices, per_device(): hc2 = lax.ppermute(hc, 'yh', SWAP)  9.16 us
    ppermute x1, waiting for transfers between devices, per_device(): gy = lax.ppermute(g, 'yl', SWAP)  9.11 us
    ppermute x6, starting transfers between devices, shift(): lax.ppermute(value, axis, [(i, (i + by) % size) for i in range(size)])  8.11 us
  transfers between devices with their start and end apart: 28, of which 13 were waited for; matrix products, arithmetic and copies ran while one was open for 2% of the time, Pallas kernels for 19%

profile of v3, /device:TPU:1, one launch (start us, length us, event | category | flops | bytes accessed | tf_op | source)
XLA Modules:
  0.0 169.9 jit_solution(5362102238841064634)
XLA Ops:
  10.5 3.8 %collective-permute-start = (bf16[480,128]{1,0:T(8,128)(2,1)S(1)}, bf16[480,128]{1,0:T(8,128)(2,1)S(1)}, u32[]{:S(2)}, u32[]{:S(2)}) collective-permute-start(bf16[480,128]{1,0:T(8,128)(2,1)S(1)} %get-tuple-element.51), channel_id=1, source_target_pairs={{0,16},{16,0},{1,17},{17,1},{2,18},{18,2},{3,19},{19,3},{4,20},{20... | collective-permute-start | bytes 368648 | tf_op jit(solution)/shard_map/ppermute | solution.py:248
  17.0 2.5 %fusion.4 = bf16[480,1792]{1,0:T(8,128)(2,1)S(1)} fusion(bf16[480,1792]{1,0:T(8,128)(2,1)} %up_pre.7, bf16[480,1792]{1,0:T(8,128)(2,1)S(1)} %copy-done.1), kind=kLoop, calls=%fused_computation.6 | loop fusion | flops 6881280 | bytes 5160960 | tf_op jit(solution)/shard_map/convert_element_type | solution.py:242
  20.3 1.9 %collective-permute-done.2 = bf16[480,128]{1,0:T(8,128)(2,1)S(1)} collective-permute-done((bf16[480,128]{1,0:T(8,128)(2,1)S(1)}, bf16[480,128]{1,0:T(8,128)(2,1)S(1)}, u32[]{:S(2)}, u32[]{:S(2)}) %collective-permute-start.2) | collective-permute-done | bytes 122912 | tf_op jit(solution)/shard_map/ppermute | solution.py:250
  25.9 9.1 %collective-permute-done.3.refs_1_ = bf16[1920,128]{1,0:T(8,128)(2,1)S(1)} collective-permute-done((bf16[1920,128]{1,0:T(8,128)(2,1)S(1)}, bf16[1920,128]{1,0:T(8,128)(2,1)S(1)}, u32[]{:S(2)}, u32[]{:S(2)}) %collective-permute-start.3) | collective-permute-done | bytes 491552 | tf_op jit(solution)/shard_map/ppermute | solution.py:257
  36.3 2.6 %collective-permute-start.11 = (bf16[480,512]{1,0:T(8,128)(2,1)S(1)}, bf16[480,512]{1,0:T(8,128)(2,1)S(1)}, u32[]{:S(2)}, u32[]{:S(2)}) collective-permute-start(bf16[480,512]{1,0:T(8,128)(2,1)S(1)} %get-tuple-element.58.refs_1_), channel_id=1, source_target_pairs={{0,16},{16,0},{1,17},{17,1},{2,18},{18,2},{3,19},{19,3},{4,20},{20... | collective-permute-start | bytes 1474568 | tf_op jit(solution)/shard_map/ppermute | solution.py:262
  43.3 6.4 %collective-permute-done.11.refs_2_ = bf16[480,512]{1,0:T(8,128)(2,1)S(1)} collective-permute-done((bf16[480,512]{1,0:T(8,128)(2,1)S(1)}, bf16[480,512]{1,0:T(8,128)(2,1)S(1)}, u32[]{:S(2)}, u32[]{:S(2)}) %collective-permute-start.11) | collective-permute-done | bytes 491552 | tf_op jit(solution)/shard_map/ppermute | solution.py:262
  51.5 2.5 %collective-permute-start.14 = (bf16[480,512]{1,0:T(8,128)(2,1)S(1)}, bf16[480,512]{1,0:T(8,128)(2,1)S(1)}, u32[]{:S(2)}, u32[]{:S(2)}) collective-permute-start(bf16[480,512]{1,0:T(8,128)(2,1)S(1)} %get-tuple-element.60.refs_5_), channel_id=1, source_target_pairs={{0,16},{16,0},{1,17},{17,1},{2,18},{18,2},{3,19},{19,3},{4,20},{20... | collective-permute-start | bytes 1474568 | tf_op jit(solution)/shard_map/ppermute | solution.py:265
  56.7 9.2 %collective-permute-done.14.refs_6_ = bf16[480,512]{1,0:T(8,128)(2,1)S(1)} collective-permute-done((bf16[480,512]{1,0:T(8,128)(2,1)S(1)}, bf16[480,512]{1,0:T(8,128)(2,1)S(1)}, u32[]{:S(2)}, u32[]{:S(2)}) %collective-permute-start.14) | collective-permute-done | bytes 491552 | tf_op jit(solution)/shard_map/ppermute | solution.py:265
  65.9 1.9 %collective-permute-done.8.refs_6_ = bf16[1920,128]{1,0:T(8,128)(2,1)S(1)} collective-permute-done((bf16[1920,128]{1,0:T(8,128)(2,1)S(1)}, bf16[1920,128]{1,0:T(8,128)(2,1)S(1)}, u32[]{:S(2)}, u32[]{:S(2)}) %collective-permute-start.8) | collective-permute-done | bytes 491552 | tf_op jit(solution)/shard_map/ppermute | solution.py:38
  71.5 6.8 %turn.1 = (bf16[1024,1920]{1,0:T(8,128)(2,1)}, bf16[960,1024]{1,0:T(8,128)(2,1)}, bf16[480,1024]{1,0:T(8,128)(2,1)}, bf16[480,1024]{1,0:T(8,128)(2,1)}) custom-call(s32[8]{0:T(128)} %stack.35.places, bf16[1920,128]{1,0:T(8,128)(2,1)} %copy-done.7, bf16[1920,128]{1,0:T(8,128)(2,1)} %copy-done.13, bf16[1920,128]{1,0:T(8,128)(2,1)} %copy-done.15, ...), custom_call_target="tpu_custom_call" | custom-call | flops 1000 | bytes 1000 | tf_op jit(solution)/shard_map/turn/pallas_call | solution.py:181
  78.9 10.5 %collective-permute-done.20.refs_10_ = bf16[480,768]{1,0:T(8,128)(2,1)} collective-permute-done((bf16[480,768]{1,0:T(8,128)(2,1)S(1)}, bf16[480,768]{1,0:T(8,128)(2,1)}, u32[]{:S(2)}, u32[]{:S(2)}) %collective-permute-start.20) | collective-permute-done | bytes 737312 | tf_op jit(solution)/shard_map/ppermute | solution.py:271
  90.3 2.4 %collective-permute-done.19.refs_8_ = bf16[480,512]{1,0:T(8,128)(2,1)S(1)} collective-permute-done((bf16[480,512]{1,0:T(8,128)(2,1)S(1)}, bf16[480,512]{1,0:T(8,128)(2,1)S(1)}, u32[]{:S(2)}, u32[]{:S(2)}) %collective-permute-start.19) | collective-permute-done | bytes 491552 | tf_op jit(solution)/shard_map/ppermute | solution.py:272
  94.2 15.1 %down_partial.1 = (bf16[1024,1792]{1,0:T(8,128)(2,1)}, s32[8]{0:T(128)}) custom-call(s32[8]{0:T(128)} %stack.35.places, bf16[1024,1920]{1,0:T(8,128)(2,1)} %get-tuple-element.71.refs_0_, bf16[480,512]{1,0:T(8,128)(2,1)} %copy-done.6, bf16[480,512]{1,0:T(8,128)(2,1)} %copy-done.12, bf16[480,512]{1,0:T(8,128)(2,1)} %copy-done.10, bf16[480,512]{1,0:T(8,128)(2,1)} %copy-done.14, ...), custom_call_target="tpu_custom_call" | custom-call | flops 1000 | bytes 1000 | tf_op jit(solution)/shard_map/down_partial/pallas_call | solution.py:84
  109.3 6.8 %hidden_partial.2 = (s32[8]{0:T(128)}, f32[480,512]{1,0:T(8,128)}, bf16[480,512]{1,0:T(8,128)(2,1)}) custom-call(s32[8]{0:T(128)} %get-tuple-element.78.places, bf16[960,1024]{1,0:T(8,128)(2,1)} %get-tuple-element.79.mine, bf16[480,1024]{1,0:T(8,128)(2,1)} %copy-done.2, bf16[480,1024]{1,0:T(8,128)(2,1)} %copy-done.3, ...), custom_call_target="tpu_custom_call" | custom-call | flops 1000 | bytes 1000 | tf_op jit(solution)/shard_map/hidden_partial/pallas_call | solution.py:147
  117.4 11.2 %hidden_partial.3 = (s32[8]{0:T(128)}, f32[480,1280]{1,0:T(8,128)}, bf16[480,512]{1,0:T(8,128)(2,1)}, bf16[480,512]{1,0:T(8,128)(2,1)}, bf16[480,256]{1,0:T(8,128)(2,1)}) custom-call(s32[8]{0:T(128)} %get-tuple-element.83.places, bf16[960,1024]{1,0:T(8,128)(2,1)} %get-tuple-element.79.mine, bf16[480,1024]{1,0:T(8,128)(2,1)} %copy-done.2, ...), custom_call_target="tpu_custom_call" | custom-call | flops 1000 | bytes 1000 | tf_op jit(solution)/shard_map/hidden_partial/pallas_call | solution.py:147
  128.6 2.1 %collective-permute-start.24 = (bf16[480,512]{1,0:T(8,128)(2,1)}, bf16[480,512]{1,0:T(8,128)(2,1)S(1)}, u32[]{:S(2)}, u32[]{:S(2)}) collective-permute-start(bf16[480,512]{1,0:T(8,128)(2,1)} %get-tuple-element.88), channel_id=1, source_target_pairs={{0,16},{16,0},{1,17},{17,1},{2,18},{18,2},{3,19},{19,3},{4,20},{20... | collective-permute-start | bytes 1474568 | tf_op jit(solution)/shard_map/ppermute | solution.py:296
  131.7 2.0 %collective-permute-start.22 = (bf16[480,256]{1,0:T(8,128)(2,1)}, bf16[480,256]{1,0:T(8,128)(2,1)S(1)}, u32[]{:S(2)}, u32[]{:S(2)}) collective-permute-start(bf16[480,256]{1,0:T(8,128)(2,1)} %get-tuple-element.85), channel_id=1, source_target_pairs={{0,16},{16,0},{1,17},{17,1},{2,18},{18,2},{3,19},{19,3},{4,20},{20... | collective-permute-start | bytes 737288 | tf_op jit(solution)/shard_map/ppermute | solution.py:296
  134.5 2.8 %finish.4 = (bf16[480,1792]{1,0:T(8,128)(2,1)}, bf16[480,1792]{1,0:T(8,128)(2,1)}) custom-call(bf16[480,1792]{1,0:T(8,128)(2,1)} %gate_pre.7, bf16[480,1792]{1,0:T(8,128)(2,1)} %up_pre.7, f32[480,512]{1,0:T(8,128)} %get-tuple-element.89.keep, bf16[480,512]{1,0:T(8,128)(2,1)} %copy-done.22), custom_call_target="tpu_custom_call" | custom-call | flops 4915200 | bytes 3932160 | tf_op jit(solution)/shard_map/finish/pallas_call | solution.py:217
  137.2 5.3 %collective-permute-done.24.far = bf16[480,512]{1,0:T(8,128)(2,1)S(1)} collective-permute-done((bf16[480,512]{1,0:T(8,128)(2,1)}, bf16[480,512]{1,0:T(8,128)(2,1)S(1)}, u32[]{:S(2)}, u32[]{:S(2)}) %collective-permute-start.24) | collective-permute-done | bytes 491552 | tf_op jit(solution)/shard_map/ppermute | solution.py:296
  143.3 2.8 %finish.5 = (bf16[480,1792]{1,0:T(8,128)(2,1)}, bf16[480,1792]{1,0:T(8,128)(2,1)}) custom-call(bf16[480,1792]{1,0:T(8,128)(2,1)} %gate_pre.7, bf16[480,1792]{1,0:T(8,128)(2,1)} %up_pre.7, f32[480,1280]{1,0:T(8,128)} %get-tuple-element.84.keep, bf16[480,512]{1,0:T(8,128)(2,1)} %copy-done.25, ...), custom_call_target="tpu_custom_call", output_to_operand_aliasing={{0}: (4, {}), {1}: (5, {})} | custom-call | flops 4915200 | bytes 3932160 | tf_op jit(solution)/shard_map/finish/pallas_call | solution.py:217
  146.1 7.0 %collective-permute-done.23.far = bf16[480,512]{1,0:T(8,128)(2,1)S(1)} collective-permute-done((bf16[480,512]{1,0:T(8,128)(2,1)}, bf16[480,512]{1,0:T(8,128)(2,1)S(1)}, u32[]{:S(2)}, u32[]{:S(2)}) %collective-permute-start.23) | collective-permute-done | bytes 491552 | tf_op jit(solution)/shard_map/ppermute | solution.py:296
  153.8 2.8 %finish.6 = (bf16[480,1792]{1,0:T(8,128)(2,1)}, bf16[480,1792]{1,0:T(8,128)(2,1)}) custom-call(bf16[480,1792]{1,0:T(8,128)(2,1)} %gate_pre.7, bf16[480,1792]{1,0:T(8,128)(2,1)} %up_pre.7, f32[480,1280]{1,0:T(8,128)} %get-tuple-element.84.keep, bf16[480,512]{1,0:T(8,128)(2,1)} %copy-done.23, ...), custom_call_target="tpu_custom_call", output_to_operand_aliasing={{0}: (4, {}), {1}: (5, {})} | custom-call | flops 4915200 | bytes 3932160 | tf_op jit(solution)/shard_map/finish/pallas_call | solution.py:217
  158.3 1.9 %reduce-scatter.2.cloned.1.call-done.refs_0_ = bf16[128,1792]{1,0:T(8,128)(2,1)} async-done(((bf16[1024,1792]{1,0:T(8,128)(2,1)}), bf16[128,1792]{1,0:T(8,128)(2,1)}) %reduce-scatter.2.cloned.1.call-update) | async-done | bytes 458768 | tf_op jit(solution)/shard_map/reduce_scatter | solution.py:288
  160.2 2.8 %finish.7 = (bf16[480,1792]{1,0:T(8,128)(2,1)}, bf16[480,1792]{1,0:T(8,128)(2,1)}, f32[128,1792]{1,0:T(8,128)}) custom-call(bf16[480,1792]{1,0:T(8,128)(2,1)} %gate_pre.7, bf16[480,1792]{1,0:T(8,128)(2,1)} %up_pre.7, f32[480,1280]{1,0:T(8,128)} %get-tuple-element.84.keep, bf16[480,256]{1,0:T(8,128)(2,1)} %copy-done.26, ...), custom_call_target="tpu_custom_call", output_to_operand_aliasing={{0}: (5, {}), {1}: (6, {})} | custom-call | flops 2457600 | bytes 1966080 | tf_op jit(solution)/shard_map/finish/pallas_call | solution.py:217
  (107 shorter events, 33.6 us)
Async XLA Ops:
  7.2 61.4 %all-gather.2.cloned.1.call-start = ((), (), s32[]{:S(2)}) async-start(), calls=%async_computation.1 | async-start | bytes 4128768 | tf_op jit(solution)/shard_map/all_gather | solution.py:255
  10.5 149.7 %reduce-scatter.2.cloned.1.call-start = ((), (), s32[]{:S(2)}) async-start(), calls=%async_computation.2 | async-start | bytes 4128768 | tf_op jit(solution)/shard_map/reduce_scatter | solution.py:288
  10.5 9.7 %collective-permute-start = (bf16[480,128]{1,0:T(8,128)(2,1)S(1)}, bf16[480,128]{1,0:T(8,128)(2,1)S(1)}, u32[]{:S(2)}, u32[]{:S(2)}) collective-permute-start(bf16[480,128]{1,0:T(8,128)(2,1)S(1)} %get-tuple-element.51), channel_id=1, source_target_pairs={{0,16},{16,0},{1,17},{17,1},{2,18},{18,2},{3,19},{19,3},{4,20},{20... | collective-permute-start | bytes 368648 | tf_op jit(solution)/shard_map/ppermute | solution.py:248
  15.3 6.9 %collective-permute-start.2 = (bf16[480,128]{1,0:T(8,128)(2,1)S(1)}, bf16[480,128]{1,0:T(8,128)(2,1)S(1)}, u32[]{:S(2)}, u32[]{:S(2)}) collective-permute-start(bf16[480,128]{1,0:T(8,128)(2,1)S(1)} %get-tuple-element.53), channel_id=1, source_target_pairs={{0,24},{8,16},{16,8},{24,0},{1,25},{9,17},{17,9},{25,1},{2,26},{10... | collective-permute-start | bytes 368648 | tf_op jit(solution)/shard_map/ppermute | solution.py:250
  22.2 12.8 %collective-permute-start.3 = (bf16[1920,128]{1,0:T(8,128)(2,1)S(1)}, bf16[1920,128]{1,0:T(8,128)(2,1)S(1)}, u32[]{:S(2)}, u32[]{:S(2)}) collective-permute-start(bf16[1920,128]{1,0:T(8,128)(2,1)S(1)} %constant_dynamic-update-slice_fusion.refs_0_), channel_id=1, source_target_pairs={{0,4},{4,0},{1,5},{5,1},{2,6},{6,2},{3,7},{7,3},{8,12},{12,8},{9,1... | collective-permute-start | bytes 1474568 | tf_op jit(solution)/shard_map/ppermute | solution.py:257
  22.3 14.0 %collective-permute-start.4 = (bf16[1920,128]{1,0:T(8,128)(2,1)S(1)}, bf16[1920,128]{1,0:T(8,128)(2,1)S(1)}, u32[]{:S(2)}, u32[]{:S(2)}) collective-permute-start(bf16[1920,128]{1,0:T(8,128)(2,1)S(1)} %constant_dynamic-update-slice_fusion.refs_0_), channel_id=1, source_target_pairs={{0,1},{1,2},{2,3},{3,0},{4,5},{5,6},{6,7},{7,4},{8,9},{9,10},{10,1... | collective-permute-start | bytes 1474568 | tf_op jit(solution)/shard_map/ppermute | solution.py:38
  23.5 12.8 %collective-permute-start.5 = (bf16[1920,128]{1,0:T(8,128)(2,1)S(1)}, bf16[1920,128]{1,0:T(8,128)(2,1)S(1)}, u32[]{:S(2)}, u32[]{:S(2)}) collective-permute-start(bf16[1920,128]{1,0:T(8,128)(2,1)S(1)} %constant_dynamic-update-slice_fusion.refs_0_), channel_id=1, source_target_pairs={{0,3},{1,0},{2,1},{3,2},{4,7},{5,4},{6,5},{7,6},{8,11},{9,8},{10,9... | collective-permute-start | bytes 1474568 | tf_op jit(solution)/shard_map/ppermute | solution.py:38
  25.1 18.2 %collective-permute-start.12 = (bf16[480,512]{1,0:T(8,128)(2,1)S(1)}, bf16[480,512]{1,0:T(8,128)(2,1)S(1)}, u32[]{:S(2)}, u32[]{:S(2)}) collective-permute-start(bf16[480,512]{1,0:T(8,128)(2,1)S(1)} %get-tuple-element.60.refs_5_), channel_id=1, source_target_pairs={{0,8},{8,0},{1,9},{9,1},{2,10},{10,2},{3,11},{11,3},{4,12},{12,4},... | collective-permute-start | bytes 1474568 | tf_op jit(solution)/shard_map/ppermute | solution.py:259
  36.3 13.4 %collective-permute-start.11 = (bf16[480,512]{1,0:T(8,128)(2,1)S(1)}, bf16[480,512]{1,0:T(8,128)(2,1)S(1)}, u32[]{:S(2)}, u32[]{:S(2)}) collective-permute-start(bf16[480,512]{1,0:T(8,128)(2,1)S(1)} %get-tuple-element.58.refs_1_), channel_id=1, source_target_pairs={{0,16},{16,0},{1,17},{17,1},{2,18},{18,2},{3,19},{19,3},{4,20},{20... | collective-permute-start | bytes 1474568 | tf_op jit(solution)/shard_map/ppermute | solution.py:262
  38.9 15.1 %collective-permute-start.7 = (bf16[1920,128]{1,0:T(8,128)(2,1)S(1)}, bf16[1920,128]{1,0:T(8,128)(2,1)S(1)}, u32[]{:S(2)}, u32[]{:S(2)}) collective-permute-start(bf16[1920,128]{1,0:T(8,128)(2,1)S(1)} %collective-permute-done.3.refs_1_), channel_id=1, source_target_pairs={{0,1},{1,2},{2,3},{3,0},{4,5},{5,6},{6,7},{7,4},{8,9},{9,10},{10,1... | collective-permute-start | bytes 1474568 | tf_op jit(solution)/shard_map/ppermute | solution.py:38
  39.7 15.2 %collective-permute-start.9 = (bf16[1920,128]{1,0:T(8,128)(2,1)S(1)}, bf16[1920,128]{1,0:T(8,128)(2,1)S(1)}, u32[]{:S(2)}, u32[]{:S(2)}) collective-permute-start(bf16[1920,128]{1,0:T(8,128)(2,1)S(1)} %collective-permute-done.3.refs_1_), channel_id=1, source_target_pairs={{0,3},{1,0},{2,1},{3,2},{4,7},{5,4},{6,5},{7,6},{8,11},{9,8},{10,9... | collective-permute-start | bytes 1474568 | tf_op jit(solution)/shard_map/ppermute | solution.py:38
  41.6 15.1 %collective-permute-start.15 = (bf16[480,768]{1,0:T(8,128)(2,1)S(1)}, bf16[480,768]{1,0:T(8,128)(2,1)S(1)}, u32[]{:S(2)}, u32[]{:S(2)}) collective-permute-start(bf16[480,768]{1,0:T(8,128)(2,1)S(1)} %slice.14.refs_9_), channel_id=1, source_target_pairs={{0,8},{8,0},{1,9},{9,1},{2,10},{10,2},{3,11},{11,3},{4,12},{12,4},... | collective-permute-start | bytes 2211848 | tf_op jit(solution)/shard_map/ppermute | solution.py:259
  49.7 7.0 %collective-permute-start.13 = (bf16[480,512]{1,0:T(8,128)(2,1)S(1)}, bf16[480,512]{1,0:T(8,128)(2,1)S(1)}, u32[]{:S(2)}, u32[]{:S(2)}) collective-permute-start(bf16[480,512]{1,0:T(8,128)(2,1)S(1)} %collective-permute-done.11.refs_2_), channel_id=1, source_target_pairs={{0,8},{8,0},{1,9},{9,1},{2,10},{10,2},{3,11},{11,3},{4,12},{12,4},... | collective-permute-start | bytes 1474568 | tf_op jit(solution)/shard_map/ppermute | solution.py:267
  51.5 14.4 %collective-permute-start.14 = (bf16[480,512]{1,0:T(8,128)(2,1)S(1)}, bf16[480,512]{1,0:T(8,128)(2,1)S(1)}, u32[]{:S(2)}, u32[]{:S(2)}) collective-permute-start(bf16[480,512]{1,0:T(8,128)(2,1)S(1)} %get-tuple-element.60.refs_5_), channel_id=1, source_target_pairs={{0,16},{16,0},{1,17},{17,1},{2,18},{18,2},{3,19},{19,3},{4,20},{20... | collective-permute-start | bytes 1474568 | tf_op jit(solution)/shard_map/ppermute | solution.py:265
  54.0 13.7 %collective-permute-start.8 = (bf16[1920,128]{1,0:T(8,128)(2,1)S(1)}, bf16[1920,128]{1,0:T(8,128)(2,1)S(1)}, u32[]{:S(2)}, u32[]{:S(2)}) collective-permute-start(bf16[1920,128]{1,0:T(8,128)(2,1)S(1)} %collective-permute-done.4.refs_2_), channel_id=1, source_target_pairs={{0,1},{1,2},{2,3},{3,0},{4,5},{5,6},{6,7},{7,4},{8,9},{9,10},{10,1... | collective-permute-start | bytes 1474568 | tf_op jit(solution)/shard_map/ppermute | solution.py:38
  54.8 13.8 %collective-permute-start.10 = (bf16[1920,128]{1,0:T(8,128)(2,1)S(1)}, bf16[1920,128]{1,0:T(8,128)(2,1)}, u32[]{:S(2)}, u32[]{:S(2)}) collective-permute-start(bf16[1920,128]{1,0:T(8,128)(2,1)S(1)} %collective-permute-done.9.refs_5_), channel_id=1, source_target_pairs={{0,3},{1,0},{2,1},{3,2},{4,7},{5,4},{6,5},{7,6},{8,11},{9,8},{10,9... | collective-permute-start | bytes 1474568 | tf_op jit(solution)/shard_map/ppermute | solution.py:38
  68.6 24.4 %collective-permute-start.16 = (bf16[1024,1792]{1,0:T(8,128)(2,1)}, bf16[1024,1792]{1,0:T(8,128)(2,1)}, u32[]{:S(2)}, u32[]{:S(2)}) collective-permute-start(bf16[1024,1792]{1,0:T(8,128)(2,1)} %all-gather.2.cloned.1.call-done.weights), channel_id=1, source_target_pairs={{0,8},{8,0},{1,9},{9,1},{2,10},{10,2},{3,11},{11,3},{4,12},{12,4},... | collective-permute-start | bytes 11010056 | tf_op jit(solution)/shard_map/ppermute | solution.py:273
  69.7 19.7 %collective-permute-start.20 = (bf16[480,768]{1,0:T(8,128)(2,1)S(1)}, bf16[480,768]{1,0:T(8,128)(2,1)}, u32[]{:S(2)}, u32[]{:S(2)}) collective-permute-start(bf16[480,768]{1,0:T(8,128)(2,1)S(1)} %slice.14.refs_9_), channel_id=1, source_target_pairs={{0,16},{16,0},{1,17},{17,1},{2,18},{18,2},{3,19},{19,3},{4,20},{20... | collective-permute-start | bytes 2211848 | tf_op jit(solution)/shard_map/ppermute | solution.py:271
  78.3 14.4 %collective-permute-start.17 = (bf16[480,1024]{1,0:T(8,128)(2,1)}, bf16[480,1024]{1,0:T(8,128)(2,1)S(1)}, u32[]{:S(2)}, u32[]{:S(2)}) collective-permute-start(bf16[480,1024]{1,0:T(8,128)(2,1)} %get-tuple-element.67), channel_id=1, source_target_pairs={{0,8},{8,0},{1,9},{9,1},{2,10},{10,2},{3,11},{11,3},{4,12},{12,4},... | collective-permute-start | bytes 2949128 | tf_op jit(solution)/shard_map/ppermute | solution.py:281
  78.7 14.0 %collective-permute-start.18 = (bf16[480,1024]{1,0:T(8,128)(2,1)}, bf16[480,1024]{1,0:T(8,128)(2,1)S(1)}, u32[]{:S(2)}, u32[]{:S(2)}) collective-permute-start(bf16[480,1024]{1,0:T(8,128)(2,1)} %get-tuple-element.68), channel_id=1, source_target_pairs={{0,8},{8,0},{1,9},{9,1},{2,10},{10,2},{3,11},{11,3},{4,12},{12,4},... | collective-permute-start | bytes 2949128 | tf_op jit(solution)/shard_map/ppermute | solution.py:281
  116.1 17.6 %collective-permute-start.25 = (bf16[480,512]{1,0:T(8,128)(2,1)}, bf16[480,512]{1,0:T(8,128)(2,1)S(1)}, u32[]{:S(2)}, u32[]{:S(2)}) collective-permute-start(bf16[480,512]{1,0:T(8,128)(2,1)} %get-tuple-element.90), channel_id=1, source_target_pairs={{0,16},{16,0},{1,17},{17,1},{2,18},{18,2},{3,19},{19,3},{4,20},{20... | collective-permute-start | bytes 1474568 | tf_op jit(solution)/shard_map/ppermute | solution.py:296
  128.6 13.9 %collective-permute-start.24 = (bf16[480,512]{1,0:T(8,128)(2,1)}, bf16[480,512]{1,0:T(8,128)(2,1)S(1)}, u32[]{:S(2)}, u32[]{:S(2)}) collective-permute-start(bf16[480,512]{1,0:T(8,128)(2,1)} %get-tuple-element.88), channel_id=1, source_target_pairs={{0,16},{16,0},{1,17},{17,1},{2,18},{18,2},{3,19},{19,3},{4,20},{20... | collective-permute-start | bytes 1474568 | tf_op jit(solution)/shard_map/ppermute | solution.py:296
  130.7 22.3 %collective-permute-start.23 = (bf16[480,512]{1,0:T(8,128)(2,1)}, bf16[480,512]{1,0:T(8,128)(2,1)S(1)}, u32[]{:S(2)}, u32[]{:S(2)}) collective-permute-start(bf16[480,512]{1,0:T(8,128)(2,1)} %get-tuple-element.87), channel_id=1, source_target_pairs={{0,16},{16,0},{1,17},{17,1},{2,18},{18,2},{3,19},{19,3},{4,20},{20... | collective-permute-start | bytes 1474568 | tf_op jit(solution)/shard_map/ppermute | solution.py:296
  131.7 26.6 %collective-permute-start.22 = (bf16[480,256]{1,0:T(8,128)(2,1)}, bf16[480,256]{1,0:T(8,128)(2,1)S(1)}, u32[]{:S(2)}, u32[]{:S(2)}) collective-permute-start(bf16[480,256]{1,0:T(8,128)(2,1)} %get-tuple-element.85), channel_id=1, source_target_pairs={{0,16},{16,0},{1,17},{17,1},{2,18},{18,2},{3,19},{19,3},{4,20},{20... | collective-permute-start | bytes 737288 | tf_op jit(solution)/shard_map/ppermute | solution.py:296
  (31 other events, 480.4 us)
Sparse Core Ops, SparseCore 0:
  10.6 53.6 all-gather.1
  109.4 50.7 reduce-scatter.1

commit v4 on v3

--- a/solution.py
+++ b/solution.py
@@ -43,61 +43,57 @@
         order[i] = places[i]
 
 
-def down_kernel(places, *refs):
-    rows, hidden = refs[0], refs[1:13]
-    out, order, turned, tall, ready, loaded, arrived, left = refs[13:]
+def down_kernel(bounds, places, *refs):
+    count = len(bounds) - 1
+    rows, hidden = refs[0], refs[1 : 1 + 4 * count]
+    out, order, turned, tall, ready, loaded, arrived, left = refs[-8:]
+    base = bounds[0]
     load = pltpu.make_async_copy(rows, turned, loaded)
     parts = [
-        [
-            pltpu.make_async_copy(
-                hidden[4 * k + r],
-                tall.at[pl.ds(r * TOK, TOK), pl.ds(PARTS[k], PARTS[k + 1] - PARTS[k])],
-                arrived.at[k, r],
-            )
-            for r in range(4)
-        ]
-        for k in range(3)
+        pltpu.make_async_copy(
+            hidden[4 * k + r],
+            tall.at[pl.ds(r * TOK, TOK), pl.ds(bounds[k] - base, bounds[k + 1] - bounds[k])],
+            arrived.at[k, r],
+        )
+        for k in range(count)
+        for r in range(4)
     ]
-    for copy in [load] + parts[0]:
+    for copy in [load] + parts:
         copy.start()
     pass_token(places, order)
-    load.wait()
-    for copy in parts[0]:
+    for copy in [load] + parts:
         copy.wait()
-    for copy in parts[1] + parts[2]:
-        copy.start()
     stores = []
     for n in range(tall.shape[1] // TILE):
-        if n * TILE in PARTS[1:]:
-            for copy in parts[PARTS.index(n * TILE)]:
-                copy.wait()
         at = pl.ds(n * TILE, TILE)
         ready[:, at] = jnp.dot(turned[...], tall[:, at], preferred_element_type=F32).astype(BF)
-        stores.append(pltpu.make_async_copy(ready.at[:, at], out.at[:, at], left.at[n]))
+        to = out.at[:, pl.ds(base + n * TILE, TILE)]
+        stores.append(pltpu.make_async_copy(ready.at[:, at], to, left.at[n]))
         stores[n].start()
     for copy in stores:
         copy.wait()
 
 
-def down_partial(places, turned, hidden):
-    cols = PARTS[-1]
+def down_partial(places, turned, hidden, bounds, made=()):
+    cols, count = bounds[-1] - bounds[0], len(bounds) - 1
     return pl.pallas_call(
-        down_kernel,
-        out_shape=(jax.ShapeDtypeStruct((8 * SIDE, cols), BF), TOKEN_TYPE),
-        in_specs=[TOKEN] + [ANY] * 13,
+        functools.partial(down_kernel, bounds),
+        out_shape=(jax.ShapeDtypeStruct((8 * SIDE, PARTS[-1]), BF), TOKEN_TYPE),
+        in_specs=[TOKEN] + [ANY] * (1 + 4 * count + len(made)),
         out_specs=(ANY, TOKEN),
+        input_output_aliases={2 + 4 * count: 0} if made else {},
         scratch_shapes=[
             pltpu.VMEM((8 * SIDE, 4 * TOK), BF),
             pltpu.VMEM((4 * TOK, cols), BF),
             pltpu.VMEM((8 * SIDE, cols), BF),
             pltpu.SemaphoreType.DMA,
-            pltpu.SemaphoreType.DMA((3, 4)),
+            pltpu.SemaphoreType.DMA((count, 4)),
             pltpu.SemaphoreType.DMA((cols // TILE,)),
         ],
         compiler_params=PARAMS,
         cost_estimate=cost(1000, 1000),
         name="down_partial",
-    )(places, turned, *hidden)
+    )(places, turned, *hidden, *made)
 
 
 def up_kernel(spans, places, mine, their_own, their_far, weights, partner_weights, *refs):
@@ -278,13 +274,15 @@
         ]
     ).astype(jnp.int32)
     turned, mine, *send = turn(places, (g, gy, g_m, g_p, gy_m, gy_p, g_far, gy_far))
+    hidden = (hb, hb2, hb1, hb3, hc, hc2, hc1, hc3)
+    down, places = down_partial(places, turned, hidden, PARTS[:3])
+    down, *send = lax.optimization_barrier((down, *send))
     theirs = [lax.ppermute(v, "c", SWAP) for v in send]
     hd3 = lax.ppermute(hd2, "c", SWAP)
-    partner_weights, turned, theirs, hc3, hd3 = lax.optimization_barrier(
-        (partner_weights, turned, theirs, hc3, hd3)
+    partner_weights, turned, theirs, down, hd3 = lax.optimization_barrier(
+        (partner_weights, turned, theirs, down, hd3)
     )
-    hidden = (hb, hb2, hb1, hb3, hc, hc2, hc1, hc3, hd, hd2, hd1, hd3)
-    down, places = down_partial(places, turned, hidden)
+    down, places = down_partial(places, turned, (hd, hd2, hd1, hd3), PARTS[2:], (down,))
     total = lax.psum_scatter(down, "z", scatter_dimension=0, tiled=True)
 
     made, found = (), []

time: 170 us -> 165 us (0.971)
  waiting for transfers between devices: 58.8 us -> 49.9 us
  Pallas kernels: 51 us -> 54.7 us
    ppermute x1, waiting for transfers between devices: 10.5 us -> 0.01 us  [per_device(): hd2 = lax.ppermute(hd, 'yh', SWAP)]
    pallas_call x1 -> x2, Pallas kernels: 15.1 us -> 18.8 us  [down_partial(): pl.pallas_call(functools.partial(down_kernel, bounds), out_shape=(jax.Sha...]
    ppermute x2, waiting for transfers between devices: 0.01 us -> 2.61 us  [per_device(): theirs = [lax.ppermute(v, 'c', SWAP) for v in send]]
    ppermute x1, waiting for transfers between devices: 2.4 us -> 0.01 us  [per_device(): hc3 = lax.ppermute(hc2, 'c', SWAP)]
    unnamed x57 -> x53, local copies, waits for them, and re-layouts: 4.41 us -> 4.13 us
  transfers between devices with their start and end apart: 28 -> 28, of which waited for: 13 -> 13; matrix products, arithmetic and copies ran while one was open for 2% -> 2% of each run, Pallas kernels for 19% -> 26%
where the time goes in v4:
time: 165 us
  Pallas kernels  54.7 us (33%)
  waiting for transfers between devices  49.9 us (30%)
  starting transfers between devices  35.2 us (21%)
  between operations  14.4 us (9%)
  local copies, waits for them, and re-layouts  6.21 us (4%)
  other arithmetic  4.37 us (3%)
    pallas_call x2, Pallas kernels, down_partial(): pl.pallas_call(functools.partial(down_kernel, bounds), out_shape=(jax.Sha...  18.8 us
    pallas_call x2, Pallas kernels, hidden_partial(): pl.pallas_call(functools.partial(up_kernel, spans), out_shape=(TOKEN_TYPE...  18 us
    ppermute x4, waiting for transfers between devices, per_device(): far = lax.ppermute(value, 'yh', SWAP)  14.7 us
    pallas_call x4, Pallas kernels, finish(): pl.pallas_call(functools.partial(finish_kernel, len(last)), out_shape=(*(...  11.2 us
    ppermute x1, waiting for transfers between devices, per_device(): hc2 = lax.ppermute(hc, 'yh', SWAP)  9.16 us
    ppermute x1, waiting for transfers between devices, per_device(): gy = lax.ppermute(g, 'yl', SWAP)  9.11 us
    ppermute x6, starting transfers between devices, shift(): lax.ppermute(value, axis, [(i, (i + by) % size) for i in range(size)])  8.11 us
    pallas_call x1, Pallas kernels, turn(): pl.pallas_call(turn_kernel, out_shape=(jax.ShapeDtypeStruct((8 * SIDE, 4...  6.72 us
  transfers between devices with their start and end apart: 28, of which 13 were waited for; matrix products, arithmetic and copies ran while one was open for 2% of the time, Pallas kernels for 26%

profile of v4, /device:TPU:1, one launch (start us, length us, event | category | flops | bytes accessed | tf_op | source)
XLA Modules:
  0.0 164.8 jit_solution(196941261176448121)
XLA Ops:
  8.6 1.9 %multiply_convert_fusion = bf16[128,1792]{1,0:T(8,128)(2,1)} fusion(bf16[128,1792]{1,0:T(8,128)(2,1)} %param.8, f32[1792]{0:T(1024)S(1)} %broadcast_bitcast_fusion), kind=kLoop, calls=%fused_computation.7 | loop fusion | flops 688128 | bytes 924672 | tf_op jit(solution)/shard_map/convert_element_type | solution.py:34
  10.5 3.8 %collective-permute-start = (bf16[480,128]{1,0:T(8,128)(2,1)S(1)}, bf16[480,128]{1,0:T(8,128)(2,1)S(1)}, u32[]{:S(2)}, u32[]{:S(2)}) collective-permute-start(bf16[480,128]{1,0:T(8,128)(2,1)S(1)} %get-tuple-element.56), channel_id=1, source_target_pairs={{0,16},{16,0},{1,17},{17,1},{2,18},{18,2},{3,19},{19,3},{4,20},{20... | collective-permute-start | bytes 368648 | tf_op jit(solution)/shard_map/ppermute | solution.py:244
  17.0 2.5 %fusion.4 = bf16[480,1792]{1,0:T(8,128)(2,1)S(1)} fusion(bf16[480,1792]{1,0:T(8,128)(2,1)} %up_pre.7, bf16[480,1792]{1,0:T(8,128)(2,1)S(1)} %copy-done.1), kind=kLoop, calls=%fused_computation.6 | loop fusion | flops 6881280 | bytes 5160960 | tf_op jit(solution)/shard_map/convert_element_type | solution.py:238
  20.3 1.9 %collective-permute-done.2 = bf16[480,128]{1,0:T(8,128)(2,1)S(1)} collective-permute-done((bf16[480,128]{1,0:T(8,128)(2,1)S(1)}, bf16[480,128]{1,0:T(8,128)(2,1)S(1)}, u32[]{:S(2)}, u32[]{:S(2)}) %collective-permute-start.2) | collective-permute-done | bytes 122912 | tf_op jit(solution)/shard_map/ppermute | solution.py:246
  25.9 9.1 %collective-permute-done.3.refs_1_ = bf16[1920,128]{1,0:T(8,128)(2,1)S(1)} collective-permute-done((bf16[1920,128]{1,0:T(8,128)(2,1)S(1)}, bf16[1920,128]{1,0:T(8,128)(2,1)S(1)}, u32[]{:S(2)}, u32[]{:S(2)}) %collective-permute-start.3) | collective-permute-done | bytes 491552 | tf_op jit(solution)/shard_map/ppermute | solution.py:253
  36.3 2.6 %collective-permute-start.11 = (bf16[480,512]{1,0:T(8,128)(2,1)S(1)}, bf16[480,512]{1,0:T(8,128)(2,1)S(1)}, u32[]{:S(2)}, u32[]{:S(2)}) collective-permute-start(bf16[480,512]{1,0:T(8,128)(2,1)S(1)} %get-tuple-element.65.refs_1_), channel_id=1, source_target_pairs={{0,16},{16,0},{1,17},{17,1},{2,18},{18,2},{3,19},{19,3},{4,20},{20... | collective-permute-start | bytes 1474568 | tf_op jit(solution)/shard_map/ppermute | solution.py:258
  39.7 1.9 %collective-permute-start.8 = (bf16[1920,128]{1,0:T(8,128)(2,1)S(1)}, bf16[1920,128]{1,0:T(8,128)(2,1)S(1)}, u32[]{:S(2)}, u32[]{:S(2)}) collective-permute-start(bf16[1920,128]{1,0:T(8,128)(2,1)S(1)} %collective-permute-done.3.refs_1_), channel_id=1, source_target_pairs={{0,3},{1,0},{2,1},{3,2},{4,7},{5,4},{6,5},{7,6},{8,11},{9,8},{10,9... | collective-permute-start | bytes 1474568 | tf_op jit(solution)/shard_map/ppermute | solution.py:38
  43.3 6.4 %collective-permute-done.11.refs_2_ = bf16[480,512]{1,0:T(8,128)(2,1)S(1)} collective-permute-done((bf16[480,512]{1,0:T(8,128)(2,1)S(1)}, bf16[480,512]{1,0:T(8,128)(2,1)S(1)}, u32[]{:S(2)}, u32[]{:S(2)}) %collective-permute-start.11) | collective-permute-done | bytes 491552 | tf_op jit(solution)/shard_map/ppermute | solution.py:258
  51.5 2.5 %collective-permute-start.14 = (bf16[480,512]{1,0:T(8,128)(2,1)S(1)}, bf16[480,512]{1,0:T(8,128)(2,1)S(1)}, u32[]{:S(2)}, u32[]{:S(2)}) collective-permute-start(bf16[480,512]{1,0:T(8,128)(2,1)S(1)} %get-tuple-element.67.refs_5_), channel_id=1, source_target_pairs={{0,16},{16,0},{1,17},{17,1},{2,18},{18,2},{3,19},{19,3},{4,20},{20... | collective-permute-start | bytes 1474568 | tf_op jit(solution)/shard_map/ppermute | solution.py:261
  54.8 1.9 %collective-permute-start.10 = (bf16[1920,128]{1,0:T(8,128)(2,1)S(1)}, bf16[1920,128]{1,0:T(8,128)(2,1)}, u32[]{:S(2)}, u32[]{:S(2)}) collective-permute-start(bf16[1920,128]{1,0:T(8,128)(2,1)S(1)} %collective-permute-done.8.refs_5_), channel_id=1, source_target_pairs={{0,3},{1,0},{2,1},{3,2},{4,7},{5,4},{6,5},{7,6},{8,11},{9,8},{10,9... | collective-permute-start | bytes 1474568 | tf_op jit(solution)/shard_map/ppermute | solution.py:38
  56.7 9.2 %collective-permute-done.14.refs_6_ = bf16[480,512]{1,0:T(8,128)(2,1)S(1)} collective-permute-done((bf16[480,512]{1,0:T(8,128)(2,1)S(1)}, bf16[480,512]{1,0:T(8,128)(2,1)S(1)}, u32[]{:S(2)}, u32[]{:S(2)}) %collective-permute-start.14) | collective-permute-done | bytes 491552 | tf_op jit(solution)/shard_map/ppermute | solution.py:261
  65.9 1.9 %collective-permute-done.9.refs_6_ = bf16[1920,128]{1,0:T(8,128)(2,1)S(1)} collective-permute-done((bf16[1920,128]{1,0:T(8,128)(2,1)S(1)}, bf16[1920,128]{1,0:T(8,128)(2,1)S(1)}, u32[]{:S(2)}, u32[]{:S(2)}) %collective-permute-start.9) | collective-permute-done | bytes 491552 | tf_op jit(solution)/shard_map/ppermute | solution.py:38
  71.5 6.7 %turn.1 = (bf16[1024,1920]{1,0:T(8,128)(2,1)}, bf16[960,1024]{1,0:T(8,128)(2,1)}, bf16[480,1024]{1,0:T(8,128)(2,1)}, bf16[480,1024]{1,0:T(8,128)(2,1)}) custom-call(s32[8]{0:T(128)} %stack.35.places, bf16[1920,128]{1,0:T(8,128)(2,1)} %copy-done.7, bf16[1920,128]{1,0:T(8,128)(2,1)} %copy-done.12, bf16[1920,128]{1,0:T(8,128)(2,1)} %copy-done.13, ...), custom_call_target="tpu_custom_call" | custom-call | flops 1000 | bytes 1000 | tf_op jit(solution)/shard_map/turn/pallas_call | solution.py:177
  78.3 10.1 %down_partial.2 = (bf16[1024,1792]{1,0:T(8,128)(2,1)}, s32[8]{0:T(128)}) custom-call(s32[8]{0:T(128)} %stack.35.places, bf16[1024,1920]{1,0:T(8,128)(2,1)} %get-tuple-element.84.refs_0_, bf16[480,512]{1,0:T(8,128)(2,1)} %copy-done.6, bf16[480,512]{1,0:T(8,128)(2,1)} %copy-done.15, bf16[480,512]{1,0:T(8,128)(2,1)} %copy-done.10, bf16[480,512]{1,0:T(8,128)(2,1)} %copy-done.18, ...), custom_call_target="tpu_custom_call" | custom-call | flops 1000 | bytes 1000 | tf_op jit(solution)/shard_map/down_partial/pallas_call | solution.py:79
  94.9 8.8 %down_partial.3 = (bf16[1024,1792]{1,0:T(8,128)(2,1)}, s32[8]{0:T(128)}) custom-call(s32[8]{0:T(128)} %get-tuple-element.75.places, bf16[1024,1920]{1,0:T(8,128)(2,1)} %get-tuple-element.84.refs_0_, bf16[480,768]{1,0:T(8,128)(2,1)} %copy-done.4, bf16[480,768]{1,0:T(8,128)(2,1)} %collective-permute-done.20.refs_2_, ...), custom_call_target="tpu_custom_call", output_to_operand_aliasing={{0}: (6, {})} | custom-call | flops 1000 | bytes 1000 | tf_op jit(solution)/shard_map/down_partial/pallas_call | solution.py:79
  103.7 6.8 %hidden_partial.2 = (s32[8]{0:T(128)}, f32[480,512]{1,0:T(8,128)}, bf16[480,512]{1,0:T(8,128)(2,1)}) custom-call(s32[8]{0:T(128)} %get-tuple-element.88.places, bf16[960,1024]{1,0:T(8,128)(2,1)} %get-tuple-element.89.mine, bf16[480,1024]{1,0:T(8,128)(2,1)} %copy-done.2, bf16[480,1024]{1,0:T(8,128)(2,1)} %copy-done.3, ...), custom_call_target="tpu_custom_call" | custom-call | flops 1000 | bytes 1000 | tf_op jit(solution)/shard_map/hidden_partial/pallas_call | solution.py:143
  110.5 2.0 %collective-permute-start.25 = (bf16[480,512]{1,0:T(8,128)(2,1)}, bf16[480,512]{1,0:T(8,128)(2,1)S(1)}, u32[]{:S(2)}, u32[]{:S(2)}) collective-permute-start(bf16[480,512]{1,0:T(8,128)(2,1)} %get-tuple-element.100), channel_id=1, source_target_pairs={{0,16},{16,0},{1,17},{17,1},{2,18},{18,2},{3,19},{19,3},{4,20},{20... | collective-permute-start | bytes 1474568 | tf_op jit(solution)/shard_map/ppermute | solution.py:294
  112.5 11.2 %hidden_partial.3 = (s32[8]{0:T(128)}, f32[480,1280]{1,0:T(8,128)}, bf16[480,512]{1,0:T(8,128)(2,1)}, bf16[480,512]{1,0:T(8,128)(2,1)}, bf16[480,256]{1,0:T(8,128)(2,1)}) custom-call(s32[8]{0:T(128)} %get-tuple-element.93.places, bf16[960,1024]{1,0:T(8,128)(2,1)} %get-tuple-element.89.mine, bf16[480,1024]{1,0:T(8,128)(2,1)} %copy-done.2, ...), custom_call_target="tpu_custom_call" | custom-call | flops 1000 | bytes 1000 | tf_op jit(solution)/shard_map/hidden_partial/pallas_call | solution.py:143
  128.8 2.8 %finish.4 = (bf16[480,1792]{1,0:T(8,128)(2,1)}, bf16[480,1792]{1,0:T(8,128)(2,1)}) custom-call(bf16[480,1792]{1,0:T(8,128)(2,1)} %gate_pre.7, bf16[480,1792]{1,0:T(8,128)(2,1)} %up_pre.7, f32[480,512]{1,0:T(8,128)} %get-tuple-element.99.keep, bf16[480,512]{1,0:T(8,128)(2,1)} %copy-done.21), custom_call_target="tpu_custom_call" | custom-call | flops 4915200 | bytes 3932160 | tf_op jit(solution)/shard_map/finish/pallas_call | solution.py:213
  131.6 6.1 %collective-permute-done.24.far = bf16[480,512]{1,0:T(8,128)(2,1)S(1)} collective-permute-done((bf16[480,512]{1,0:T(8,128)(2,1)}, bf16[480,512]{1,0:T(8,128)(2,1)S(1)}, u32[]{:S(2)}, u32[]{:S(2)}) %collective-permute-start.24) | collective-permute-done | bytes 491552 | tf_op jit(solution)/shard_map/ppermute | solution.py:294
  138.4 2.8 %finish.5 = (bf16[480,1792]{1,0:T(8,128)(2,1)}, bf16[480,1792]{1,0:T(8,128)(2,1)}) custom-call(bf16[480,1792]{1,0:T(8,128)(2,1)} %gate_pre.7, bf16[480,1792]{1,0:T(8,128)(2,1)} %up_pre.7, f32[480,1280]{1,0:T(8,128)} %get-tuple-element.94.keep, bf16[480,512]{1,0:T(8,128)(2,1)} %copy-done.23, ...), custom_call_target="tpu_custom_call", output_to_operand_aliasing={{0}: (4, {}), {1}: (5, {})} | custom-call | flops 4915200 | bytes 3932160 | tf_op jit(solution)/shard_map/finish/pallas_call | solution.py:213
  141.3 6.9 %collective-permute-done.23.far = bf16[480,512]{1,0:T(8,128)(2,1)S(1)} collective-permute-done((bf16[480,512]{1,0:T(8,128)(2,1)}, bf16[480,512]{1,0:T(8,128)(2,1)S(1)}, u32[]{:S(2)}, u32[]{:S(2)}) %collective-permute-start.23) | collective-permute-done | bytes 491552 | tf_op jit(solution)/shard_map/ppermute | solution.py:294
  149.0 2.8 %finish.6 = (bf16[480,1792]{1,0:T(8,128)(2,1)}, bf16[480,1792]{1,0:T(8,128)(2,1)}) custom-call(bf16[480,1792]{1,0:T(8,128)(2,1)} %gate_pre.7, bf16[480,1792]{1,0:T(8,128)(2,1)} %up_pre.7, f32[480,1280]{1,0:T(8,128)} %get-tuple-element.94.keep, bf16[480,512]{1,0:T(8,128)(2,1)} %copy-done.22, ...), custom_call_target="tpu_custom_call", output_to_operand_aliasing={{0}: (4, {}), {1}: (5, {})} | custom-call | flops 4915200 | bytes 3932160 | tf_op jit(solution)/shard_map/finish/pallas_call | solution.py:213
  155.1 2.8 %finish.7 = (bf16[480,1792]{1,0:T(8,128)(2,1)}, bf16[480,1792]{1,0:T(8,128)(2,1)}, f32[128,1792]{1,0:T(8,128)}) custom-call(bf16[480,1792]{1,0:T(8,128)(2,1)} %gate_pre.7, bf16[480,1792]{1,0:T(8,128)(2,1)} %up_pre.7, f32[480,1280]{1,0:T(8,128)} %get-tuple-element.94.keep, bf16[480,256]{1,0:T(8,128)(2,1)} %copy-done.24, ...), custom_call_target="tpu_custom_call", output_to_operand_aliasing={{0}: (5, {}), {1}: (6, {})} | custom-call | flops 2457600 | bytes 1966080 | tf_op jit(solution)/shard_map/finish/pallas_call | solution.py:213
  (104 shorter events, 35.2 us)
Async XLA Ops:
  7.2 61.4 %all-gather.2.cloned.1.call-start = ((), (), s32[]{:S(2)}) async-start(), calls=%async_computation.1 | async-start | bytes 4128768 | tf_op jit(solution)/shard_map/all_gather | solution.py:251
  10.5 144.7 %reduce-scatter.2.cloned.1.call-start = ((), (), s32[]{:S(2)}) async-start(), calls=%async_computation.2 | async-start | bytes 4128768 | tf_op jit(solution)/shard_map/reduce_scatter | solution.py:286
  10.5 9.7 %collective-permute-start = (bf16[480,128]{1,0:T(8,128)(2,1)S(1)}, bf16[480,128]{1,0:T(8,128)(2,1)S(1)}, u32[]{:S(2)}, u32[]{:S(2)}) collective-permute-start(bf16[480,128]{1,0:T(8,128)(2,1)S(1)} %get-tuple-element.56), channel_id=1, source_target_pairs={{0,16},{16,0},{1,17},{17,1},{2,18},{18,2},{3,19},{19,3},{4,20},{20... | collective-permute-start | bytes 368648 | tf_op jit(solution)/shard_map/ppermute | solution.py:244
  15.3 6.9 %collective-permute-start.2 = (bf16[480,128]{1,0:T(8,128)(2,1)S(1)}, bf16[480,128]{1,0:T(8,128)(2,1)S(1)}, u32[]{:S(2)}, u32[]{:S(2)}) collective-permute-start(bf16[480,128]{1,0:T(8,128)(2,1)S(1)} %get-tuple-element.58), channel_id=1, source_target_pairs={{0,24},{8,16},{16,8},{24,0},{1,25},{9,17},{17,9},{25,1},{2,26},{10... | collective-permute-start | bytes 368648 | tf_op jit(solution)/shard_map/ppermute | solution.py:246
  19.6 6.3 %collective-permute-start.6 = (bf16[480,512]{1,0:T(8,128)(2,1)S(1)}, bf16[480,512]{1,0:T(8,128)(2,1)S(1)}, u32[]{:S(2)}, u32[]{:S(2)}) collective-permute-start(bf16[480,512]{1,0:T(8,128)(2,1)S(1)} %get-tuple-element.65.refs_1_), channel_id=1, source_target_pairs={{0,8},{8,0},{1,9},{9,1},{2,10},{10,2},{3,11},{11,3},{4,12},{12,4},... | collective-permute-start | bytes 1474568 | tf_op jit(solution)/shard_map/ppermute | solution.py:255
  22.2 12.8 %collective-permute-start.3 = (bf16[1920,128]{1,0:T(8,128)(2,1)S(1)}, bf16[1920,128]{1,0:T(8,128)(2,1)S(1)}, u32[]{:S(2)}, u32[]{:S(2)}) collective-permute-start(bf16[1920,128]{1,0:T(8,128)(2,1)S(1)} %constant_dynamic-update-slice_fusion.refs_0_), channel_id=1, source_target_pairs={{0,4},{4,0},{1,5},{5,1},{2,6},{6,2},{3,7},{7,3},{8,12},{12,8},{9,1... | collective-permute-start | bytes 1474568 | tf_op jit(solution)/shard_map/ppermute | solution.py:253
  22.3 14.0 %collective-permute-start.4 = (bf16[1920,128]{1,0:T(8,128)(2,1)S(1)}, bf16[1920,128]{1,0:T(8,128)(2,1)S(1)}, u32[]{:S(2)}, u32[]{:S(2)}) collective-permute-start(bf16[1920,128]{1,0:T(8,128)(2,1)S(1)} %constant_dynamic-update-slice_fusion.refs_0_), channel_id=1, source_target_pairs={{0,1},{1,2},{2,3},{3,0},{4,5},{5,6},{6,7},{7,4},{8,9},{9,10},{10,1... | collective-permute-start | bytes 1474568 | tf_op jit(solution)/shard_map/ppermute | solution.py:38
  23.5 12.8 %collective-permute-start.5 = (bf16[1920,128]{1,0:T(8,128)(2,1)S(1)}, bf16[1920,128]{1,0:T(8,128)(2,1)S(1)}, u32[]{:S(2)}, u32[]{:S(2)}) collective-permute-start(bf16[1920,128]{1,0:T(8,128)(2,1)S(1)} %constant_dynamic-update-slice_fusion.refs_0_), channel_id=1, source_target_pairs={{0,3},{1,0},{2,1},{3,2},{4,7},{5,4},{6,5},{7,6},{8,11},{9,8},{10,9... | collective-permute-start | bytes 1474568 | tf_op jit(solution)/shard_map/ppermute | solution.py:38
  25.1 18.2 %collective-permute-start.12 = (bf16[480,512]{1,0:T(8,128)(2,1)S(1)}, bf16[480,512]{1,0:T(8,128)(2,1)S(1)}, u32[]{:S(2)}, u32[]{:S(2)}) collective-permute-start(bf16[480,512]{1,0:T(8,128)(2,1)S(1)} %get-tuple-element.67.refs_5_), channel_id=1, source_target_pairs={{0,8},{8,0},{1,9},{9,1},{2,10},{10,2},{3,11},{11,3},{4,12},{12,4},... | collective-permute-start | bytes 1474568 | tf_op jit(solution)/shard_map/ppermute | solution.py:255
  36.3 13.4 %collective-permute-start.11 = (bf16[480,512]{1,0:T(8,128)(2,1)S(1)}, bf16[480,512]{1,0:T(8,128)(2,1)S(1)}, u32[]{:S(2)}, u32[]{:S(2)}) collective-permute-start(bf16[480,512]{1,0:T(8,128)(2,1)S(1)} %get-tuple-element.65.refs_1_), channel_id=1, source_target_pairs={{0,16},{16,0},{1,17},{17,1},{2,18},{18,2},{3,19},{19,3},{4,20},{20... | collective-permute-start | bytes 1474568 | tf_op jit(solution)/shard_map/ppermute | solution.py:258
  38.9 15.1 %collective-permute-start.7 = (bf16[1920,128]{1,0:T(8,128)(2,1)S(1)}, bf16[1920,128]{1,0:T(8,128)(2,1)S(1)}, u32[]{:S(2)}, u32[]{:S(2)}) collective-permute-start(bf16[1920,128]{1,0:T(8,128)(2,1)S(1)} %collective-permute-done.3.refs_1_), channel_id=1, source_target_pairs={{0,1},{1,2},{2,3},{3,0},{4,5},{5,6},{6,7},{7,4},{8,9},{9,10},{10,1... | collective-permute-start | bytes 1474568 | tf_op jit(solution)/shard_map/ppermute | solution.py:38
  39.7 15.2 %collective-permute-start.8 = (bf16[1920,128]{1,0:T(8,128)(2,1)S(1)}, bf16[1920,128]{1,0:T(8,128)(2,1)S(1)}, u32[]{:S(2)}, u32[]{:S(2)}) collective-permute-start(bf16[1920,128]{1,0:T(8,128)(2,1)S(1)} %collective-permute-done.3.refs_1_), channel_id=1, source_target_pairs={{0,3},{1,0},{2,1},{3,2},{4,7},{5,4},{6,5},{7,6},{8,11},{9,8},{10,9... | collective-permute-start | bytes 1474568 | tf_op jit(solution)/shard_map/ppermute | solution.py:38
  41.6 15.1 %collective-permute-start.15 = (bf16[480,768]{1,0:T(8,128)(2,1)S(1)}, bf16[480,768]{1,0:T(8,128)(2,1)S(1)}, u32[]{:S(2)}, u32[]{:S(2)}) collective-permute-start(bf16[480,768]{1,0:T(8,128)(2,1)S(1)} %slice.14.refs_1_), channel_id=1, source_target_pairs={{0,8},{8,0},{1,9},{9,1},{2,10},{10,2},{3,11},{11,3},{4,12},{12,4},... | collective-permute-start | bytes 2211848 | tf_op jit(solution)/shard_map/ppermute | solution.py:255
  49.7 7.0 %collective-permute-start.13 = (bf16[480,512]{1,0:T(8,128)(2,1)S(1)}, bf16[480,512]{1,0:T(8,128)(2,1)S(1)}, u32[]{:S(2)}, u32[]{:S(2)}) collective-permute-start(bf16[480,512]{1,0:T(8,128)(2,1)S(1)} %collective-permute-done.11.refs_2_), channel_id=1, source_target_pairs={{0,8},{8,0},{1,9},{9,1},{2,10},{10,2},{3,11},{11,3},{4,12},{12,4},... | collective-permute-start | bytes 1474568 | tf_op jit(solution)/shard_map/ppermute | solution.py:263
  51.5 14.4 %collective-permute-start.14 = (bf16[480,512]{1,0:T(8,128)(2,1)S(1)}, bf16[480,512]{1,0:T(8,128)(2,1)S(1)}, u32[]{:S(2)}, u32[]{:S(2)}) collective-permute-start(bf16[480,512]{1,0:T(8,128)(2,1)S(1)} %get-tuple-element.67.refs_5_), channel_id=1, source_target_pairs={{0,16},{16,0},{1,17},{17,1},{2,18},{18,2},{3,19},{19,3},{4,20},{20... | collective-permute-start | bytes 1474568 | tf_op jit(solution)/shard_map/ppermute | solution.py:261
  54.0 13.7 %collective-permute-start.9 = (bf16[1920,128]{1,0:T(8,128)(2,1)S(1)}, bf16[1920,128]{1,0:T(8,128)(2,1)S(1)}, u32[]{:S(2)}, u32[]{:S(2)}) collective-permute-start(bf16[1920,128]{1,0:T(8,128)(2,1)S(1)} %collective-permute-done.4.refs_2_), channel_id=1, source_target_pairs={{0,1},{1,2},{2,3},{3,0},{4,5},{5,6},{6,7},{7,4},{8,9},{9,10},{10,1... | collective-permute-start | bytes 1474568 | tf_op jit(solution)/shard_map/ppermute | solution.py:38
  54.8 13.8 %collective-permute-start.10 = (bf16[1920,128]{1,0:T(8,128)(2,1)S(1)}, bf16[1920,128]{1,0:T(8,128)(2,1)}, u32[]{:S(2)}, u32[]{:S(2)}) collective-permute-start(bf16[1920,128]{1,0:T(8,128)(2,1)S(1)} %collective-permute-done.8.refs_5_), channel_id=1, source_target_pairs={{0,3},{1,0},{2,1},{3,2},{4,7},{5,4},{6,5},{7,6},{8,11},{9,8},{10,9... | collective-permute-start | bytes 1474568 | tf_op jit(solution)/shard_map/ppermute | solution.py:38
  68.6 25.4 %collective-permute-start.17 = (bf16[1024,1792]{1,0:T(8,128)(2,1)}, bf16[1024,1792]{1,0:T(8,128)(2,1)}, u32[]{:S(2)}, u32[]{:S(2)}) collective-permute-start(bf16[1024,1792]{1,0:T(8,128)(2,1)} %all-gather.2.cloned.1.call-done.weights), channel_id=1, source_target_pairs={{0,8},{8,0},{1,9},{9,1},{2,10},{10,2},{3,11},{11,3},{4,12},{12,4},... | collective-permute-start | bytes 11010056 | tf_op jit(solution)/shard_map/ppermute | solution.py:269
  69.7 8.5 %collective-permute-start.16 = (bf16[480,512]{1,0:T(8,128)(2,1)}, bf16[480,512]{1,0:T(8,128)(2,1)}, u32[]{:S(2)}, u32[]{:S(2)}) collective-permute-start(bf16[480,512]{1,0:T(8,128)(2,1)} %copy-done.19), channel_id=1, source_target_pairs={{0,8},{8,0},{1,9},{9,1},{2,10},{10,2},{3,11},{11,3},{4,12},{12,4},... | collective-permute-start | bytes 1474568 | tf_op jit(solution)/shard_map/ppermute | solution.py:268
  69.8 19.4 %collective-permute-start.20 = (bf16[480,768]{1,0:T(8,128)(2,1)S(1)}, bf16[480,768]{1,0:T(8,128)(2,1)}, u32[]{:S(2)}, u32[]{:S(2)}) collective-permute-start(bf16[480,768]{1,0:T(8,128)(2,1)S(1)} %slice.14.refs_1_), channel_id=1, source_target_pairs={{0,16},{16,0},{1,17},{17,1},{2,18},{18,2},{3,19},{19,3},{4,20},{20... | collective-permute-start | bytes 2211848 | tf_op jit(solution)/shard_map/ppermute | solution.py:267
  110.5 17.5 %collective-permute-start.25 = (bf16[480,512]{1,0:T(8,128)(2,1)}, bf16[480,512]{1,0:T(8,128)(2,1)S(1)}, u32[]{:S(2)}, u32[]{:S(2)}) collective-permute-start(bf16[480,512]{1,0:T(8,128)(2,1)} %get-tuple-element.100), channel_id=1, source_target_pairs={{0,16},{16,0},{1,17},{17,1},{2,18},{18,2},{3,19},{19,3},{4,20},{20... | collective-permute-start | bytes 1474568 | tf_op jit(solution)/shard_map/ppermute | solution.py:294
  123.8 13.9 %collective-permute-start.24 = (bf16[480,512]{1,0:T(8,128)(2,1)}, bf16[480,512]{1,0:T(8,128)(2,1)S(1)}, u32[]{:S(2)}, u32[]{:S(2)}) collective-permute-start(bf16[480,512]{1,0:T(8,128)(2,1)} %get-tuple-element.98), channel_id=1, source_target_pairs={{0,16},{16,0},{1,17},{17,1},{2,18},{18,2},{3,19},{19,3},{4,20},{20... | collective-permute-start | bytes 1474568 | tf_op jit(solution)/shard_map/ppermute | solution.py:294
  125.0 23.2 %collective-permute-start.23 = (bf16[480,512]{1,0:T(8,128)(2,1)}, bf16[480,512]{1,0:T(8,128)(2,1)S(1)}, u32[]{:S(2)}, u32[]{:S(2)}) collective-permute-start(bf16[480,512]{1,0:T(8,128)(2,1)} %get-tuple-element.97), channel_id=1, source_target_pairs={{0,16},{16,0},{1,17},{17,1},{2,18},{18,2},{3,19},{19,3},{4,20},{20... | collective-permute-start | bytes 1474568 | tf_op jit(solution)/shard_map/ppermute | solution.py:294
  126.8 26.6 %collective-permute-start.22 = (bf16[480,256]{1,0:T(8,128)(2,1)}, bf16[480,256]{1,0:T(8,128)(2,1)S(1)}, u32[]{:S(2)}, u32[]{:S(2)}) collective-permute-start(bf16[480,256]{1,0:T(8,128)(2,1)} %get-tuple-element.95), channel_id=1, source_target_pairs={{0,16},{16,0},{1,17},{17,1},{2,18},{18,2},{3,19},{19,3},{4,20},{20... | collective-permute-start | bytes 737288 | tf_op jit(solution)/shard_map/ppermute | solution.py:294
  (29 other events, 510.6 us)
Sparse Core Ops, SparseCore 0:
  10.6 53.6 all-gather.1
  103.8 51.2 reduce-scatter.1
